TPU v7x, 32 devices: a whole 2x2x4 slice. The times are simulated.
32 devices in a mesh: dp: 8 (over y, x, core), mp: 4 (over z).
Axes of the slice: x: 2, y: 2, z: 4, core: 2. Of those that a mesh axis runs over, the one named last changes fastest.
Arguments:
- sequence: bfloat16 [128, 532, 512], P(('dp', 'mp')), may hold values from -6 to 6
- cotangent: bfloat16 [128, 532, 512], P(('dp', 'mp')), may hold values from -6 to 6
- w_query: bfloat16 [512, 512], replicated, may hold values from -0.25 to 0.25
- b_query: bfloat16 [512], replicated, may hold values from -2.5 to 2.5
- w_key: bfloat16 [512, 512], replicated, may hold values from -0.25 to 0.25
- w_value: bfloat16 [512, 512], replicated, may hold values from -0.25 to 0.25
- b_value: bfloat16 [512], replicated, may hold values from -2.5 to 2.5
- w_out: bfloat16 [512, 512], replicated, may hold values from -1.5 to 1.5
- b_out: bfloat16 [512], replicated, may hold values from -2.5 to 2.5
- gain_attn: bfloat16 [512], replicated, may hold values from 0.5 to 1.5
- shift_attn: bfloat16 [512], replicated, may hold values from -2.5 to 2.5
- w_in: bfloat16 [512, 2048], P(None, 'mp'), may hold values from -0.25 to 0.25
- b_in: bfloat16 [2048], P('mp'), may hold values from -2.5 to 2.5
- w_back: bfloat16 [2048, 512], P('mp'), may hold values from -0.125 to 0.125
- b_back: bfloat16 [512], replicated, may hold values from -2.5 to 2.5
- gain_ffn: bfloat16 [512], replicated, may hold values from 0.5 to 1.5
- shift_ffn: bfloat16 [512], replicated, may hold values from -2.5 to 2.5
Outputs:
- layer_out: bfloat16 [128, 532, 512], P(('dp', 'mp'))
- input_grad: float32 [128, 532, 512], P(('dp', 'mp'))
- grad_w_query: float32 [512, 512], P('mp')
- grad_b_query: float32 [512], P('mp')
- grad_w_key: float32 [512, 512], P('mp')
- grad_w_value: float32 [512, 512], P('mp')
- grad_b_value: float32 [512], P('mp')
- grad_w_out: float32 [512, 512], P('mp')
- grad_b_out: float32 [512], P('mp')
- grad_gain_attn: float32 [512], P('mp')
- grad_shift_attn: float32 [512], P('mp')
- grad_w_in: float32 [512, 2048], P(None, 'mp')
- grad_b_in: float32 [2048], P('mp')
- grad_w_back: float32 [2048, 512], P('mp')
- grad_b_back: float32 [512], P('mp')
- grad_gain_ffn: float32 [512], P('mp')
- grad_shift_ffn: float32 [512], P('mp')
All inputs are finite; a program needn't handle non-finite values.
Results may differ from a plain program's by a relative error of at most 0.019.
Values may be sent and summed in bfloat16 or wider, within the bound.
No kernel may reach another device: no remote copies, remote signals or barrier semaphores. Data moves between devices by JAX's collectives and lax.ppermute only.
A program may use at most 192 MiB of HBM per device.

v0:
```python
import functools

import jax
import jax.numpy as jnp
from jax import lax
from jax.experimental import pallas as pl
from jax.experimental.pallas import tpu as pltpu
from jax.sharding import PartitionSpec as P

HEADS = 8
GROUPS = 2
INNER = 8
NEG = -1e30
C0 = (2.0 / 3.141592653589793) ** 0.5
C1 = C0 * 0.044715
LOG2E = 1.4426950408889634
f32 = jnp.float32
bf16 = jnp.bfloat16


def dot(left, right, a, b):
    return lax.dot_general(left, right, (((a,), (b,)), ((), ())), preferred_element_type=f32)


def nn(left, right):
    return dot(left, right, 1, 0)


def nt(left, right):
    return dot(left, right, 1, 1)


def tn(left, right):
    return dot(left, right, 0, 0)


def fold(v):
    return jnp.sum(v.reshape(v.shape[0] // 8, 8, v.shape[1]), 0)


def row_mean(v):
    return jnp.mean(v, -1, keepdims=True)


def lanes(n):
    return (n + 127) // 128 * 128


def cost(us):
    return pl.CostEstimate(flops=int(us * 1e9), bytes_accessed=int(us * 1e5), transcendentals=0)


def params(mib=60):
    return pltpu.CompilerParams(vmem_limit_bytes=mib * 2**20)


def whole(a):
    return pl.BlockSpec(a.shape, lambda *_: (0,) * len(a.shape), pipeline_mode=pl.Buffered(1))


ANY = pl.BlockSpec(memory_space=pl.ANY)


def shape(dims, dtype):
    return jax.ShapeDtypeStruct(tuple(dims), dtype)


def prep_body(at_ref, wi_ref, wb_ref, bi_ref, piece_ref):
    a, b = wi_ref.shape[0], wb_ref.shape[0]
    piece_ref[:a, :] = wi_ref[...]
    piece_ref[a : a + b, :] = wb_ref[...]
    bias = bi_ref[...].astype(f32).reshape(1, -1)
    piece_ref[a + b :, :] = jnp.concatenate([bias, jnp.zeros((15, bias.shape[1]), f32)], 0).astype(bf16)


def prep(at, wi, wb, bi):
    width, own = wi.shape
    a, b = width // INNER, own // INNER
    return pl.pallas_call(
        prep_body,
        grid_spec=pltpu.PrefetchScalarGridSpec(
            num_scalar_prefetch=1,
            grid=(1,),
            in_specs=[pl.BlockSpec((a, own), lambda i, at: (at[0], 0)), pl.BlockSpec((b, width), lambda i, at: (at[0], 0)), whole(bi)],
            out_specs=pl.BlockSpec((a + b + 16, width), lambda *_: (0, 0)),
        ),
        out_shape=shape((a + b + 16, width), bf16),
        compiler_params=params(),
        cost_estimate=cost(2),
        name="prep",
    )(at, wi, wb, bi)


def vectors_body(*refs):
    for j, v in enumerate(refs[:8]):
        refs[-1][j : j + 1, :] = v[...].astype(f32).reshape(1, -1)


def stack_vectors(vectors, after):
    return pl.pallas_call(
        vectors_body,
        in_specs=[pl.BlockSpec(memory_space=pltpu.VMEM)] * 8 + [ANY] * len(after),
        out_specs=pl.BlockSpec(memory_space=pltpu.VMEM),
        out_shape=shape((8, vectors[0].shape[0]), f32),
        cost_estimate=cost(1),
        name="vectors",
    )(*vectors, *after)


def attend_body(rows, pad, skip, x_ref, wq_ref, wk_ref, wv_ref, wo_ref, vec_ref, *refs):
    qt_ref, k_ref, v_ref, mt_ref, lt_ref, so_ref, xp, vt = refs[skip:]
    width = x_ref.shape[-1]
    hs = width // HEADS
    main = rows // 128 * 128
    left = pad - main
    group = 128 // left
    top = rows // 16 * 16

    @pl.when(pl.program_id(0) == 0)
    def _():
        xp[top:, :] = jnp.zeros((pad - top, width), bf16)

    xp[:rows, :] = x_ref[0]
    x = xp[...]
    scale = hs**-0.5
    qt_ref[0, :, :pad] = ((nn(x, wq_ref[...]) + vec_ref[0:1, :]) * (scale * LOG2E)).astype(bf16).T
    k_ref[0] = nn(x, wk_ref[...]).astype(bf16)
    v = (nn(x, wv_ref[...]) + vec_ref[1:2, :]).astype(bf16)
    v_ref[0] = v
    vt[...] = v.T
    valid = lax.broadcasted_iota(jnp.int32, (pad - top, 1), 0) < rows - top
    ones = jnp.ones((16, pad), bf16)

    def soft(st):
        s_top = st[:top]
        s_bot = jnp.where(valid, st[top:], NEG)
        m = jnp.maximum(jnp.max(s_top, 0, keepdims=True), jnp.max(s_bot, 0, keepdims=True))
        p = jnp.concatenate([jnp.exp2(s_top - m).astype(bf16), jnp.exp2(s_bot - m).astype(bf16)], 0)
        return m, p

    cs = [slice(hs * h, hs * h + hs) for h in range(HEADS)]
    following = nn(k_ref[0, :, cs[0]], qt_ref[0, cs[0], :main])
    for h in range(HEADS):
        c = cs[h]
        st = following
        if h + 1 < HEADS:
            following = nn(k_ref[0, :, cs[h + 1]], qt_ref[0, cs[h + 1], :main])
        m, p = soft(st)
        ot = nn(jnp.concatenate([vt[c, :], ones], 0), p)
        total = ot[hs : hs + 1]
        mt_ref[0, c, :main] = (ot[:hs] * (1.0 / total)).astype(bf16)
        lt_ref[0, h // (HEADS // GROUPS), h % (HEADS // GROUPS) : h % (HEADS // GROUPS) + 1, :main] = m + jnp.log2(total)
    for g in range(HEADS // group):
        w = hs * group
        c = slice(w * g, w * g + w)
        same = (lax.broadcasted_iota(jnp.int32, (w, 128), 0) // hs
                == lax.broadcasted_iota(jnp.int32, (w, 128), 1) // left)
        ql = jnp.where(same, jnp.concatenate([qt_ref[0, c, main:pad]] * group, 1), 0).astype(bf16)
        m, p = soft(nn(k_ref[0, :, c], ql))
        ot = nn(jnp.concatenate([vt[c, :], ones], 0), p)
        total = ot[w : w + 1]
        o = ot[:w] * (1.0 / total)
        lt = m + jnp.log2(total)
        for j in range(group):
            h = g * group + j
            mt_ref[0, hs * h : hs * h + hs, main:pad] = o[hs * j : hs * j + hs, left * j : left * j + left].astype(bf16)
            lt_ref[0, h // (HEADS // GROUPS), h % (HEADS // GROUPS) : h % (HEADS // GROUPS) + 1, main:pad] = lt[:, left * j : left * j + left]
    so_ref[0] = tn(mt_ref[0, :, :pad], wo_ref[...]) + vec_ref[2:3, :] + xp[...].astype(f32)


def attend(sequence, wq, wk, wv, wo, vec, first, count, before=(), after=()):
    spans, rows, width = sequence.shape
    pad = (rows + 31) // 32 * 32
    wide = lanes(pad)
    per = HEADS // GROUPS
    spec = lambda a, b: pl.BlockSpec((1, a, b), lambda i: (i + first, 0, 0))
    return pl.pallas_call(
        functools.partial(attend_body, rows, pad, len(before) + len(after)),
        grid=(count,),
        in_specs=[spec(rows, width)] + [whole(w) for w in (wq, wk, wv, wo, vec)] + [ANY] * (len(before) + len(after)),
        out_specs=[spec(width, wide), spec(pad, width), spec(pad, width), spec(width, wide),
                   pl.BlockSpec((1, GROUPS, per, wide), lambda i: (i + first, 0, 0, 0)), spec(pad, width)],
        out_shape=[shape((spans, width, wide), bf16), shape((spans, pad, width), bf16), shape((spans, pad, width), bf16),
                   shape((spans, width, wide), bf16), shape((spans, GROUPS, per, wide), f32), shape((spans, pad, width), f32)],
        scratch_shapes=[pltpu.VMEM((pad, width), bf16), pltpu.VMEM((width, pad), bf16)],
        input_output_aliases={6 + n: n for n in range(len(before))},
        compiler_params=params(),
        cost_estimate=cost(16),
        name=f"attend{first}",
    )(sequence, wq, wk, wv, wo, vec, *before, *after)


def vector_rows(vec, slot, count):
    mine = lax.broadcasted_iota(jnp.int32, vec.shape, 0) == slot
    row = jnp.sum(jnp.where(mine, vec, 0.0), 0, keepdims=True)
    return jnp.concatenate([row, jnp.zeros((count - 1, vec.shape[1]), f32)], 0)


def ffn_body(rows, slices, planes, at_ref, so_ref, ct_ref, mt_ref, vec_ref, wo_ref, bi_ref, bf_ref, wi_ref, wb_ref, *refs):
    (lo_ref, gs_ref, ga_ref, dot_ref, o0_ref, o1_ref,
     col, binv, wi, wb, one, two, inv1, act, pre_grad, low, grad, acc, turn, sem) = refs[slices:]
    pad, width = so_ref.shape[1:]
    own = wb_ref.shape[0]
    hidden = wb.shape[0]
    cut_in, cut_back = width // INNER, own // INNER
    step = pl.program_id(0)

    def slot_of(half, hi):
        return at_ref[0] ^ (half + 2 * hi)

    def loads():
        copies = [pltpu.make_async_copy(wi_ref, wi.at[:, :own], sem.at[0]),
                  pltpu.make_async_copy(wb_ref, wb.at[:own, :], sem.at[1])]
        for q in range(slices):
            slot = slot_of(q // (INNER // 2), q % (INNER // 2))
            for s in range(1, planes):
                n = 2 + 2 * (q * (planes - 1) + s - 1)
                there = wi.at[pl.ds(pl.multiple_of(slot * cut_in, cut_in), cut_in), own * s : own * s + own]
                copies.append(pltpu.make_async_copy(refs[q].at[s - 1, :cut_in, :], there, sem.at[n]))
                there = wb.at[pl.ds(pl.multiple_of(own * s + slot * cut_back, cut_back), cut_back), :]
                copies.append(pltpu.make_async_copy(refs[q].at[s - 1, cut_in : cut_in + cut_back, :], there, sem.at[n + 1]))
        return copies

    @pl.when(step == 0)
    def _():
        for c in loads():
            c.start()
        col[...] = jnp.zeros_like(col)
        binv[...] = jnp.zeros_like(binv)
        acc[...] = jnp.zeros_like(acc)

    bb, g1, s1, g2, s2 = (vec_ref[n : n + 1, :] for n in range(3, 8))
    base = pl.multiple_of(step * pad, pad)
    unit = own
    chunks = [slice(n, n + unit) for n in range(0, hidden, unit)]
    bias = [bi_ref[...].astype(f32).reshape(1, -1)] + [bf_ref[s : s + 1, :] for s in range(planes - 1)]
    zero = [jnp.zeros((8, width), f32)] * 3

    def chain(first, size, tall):
        here = pl.ds(pl.multiple_of(base + first, 16), size)
        blocks = [slice(first + n, first + n + tall) for n in range(0, size, tall)]
        local = lambda b: slice(b.start - first, b.stop - first)
        there = lambda b: pl.ds(pl.multiple_of(base + b.start, 16), tall)

        def norm():
            for b in blocks:
                r = so_ref[0, b, :]
                c = r - row_mean(r)
                inv = lax.rsqrt(row_mean(c * c) + 1e-5)
                unit1 = c * inv
                one[b, :] = unit1
                inv1[b, :] = jnp.broadcast_to(inv, (tall, 128))
                low[there(b), :] = (unit1 * g1 + s1).astype(bf16)

        def hidden_units():
            nl = low[here, :]
            for cs, add_bias in zip(chunks, bias):
                pre = nn(nl, wi[:, cs])
                for b in blocks:
                    v = pre[local(b)] + add_bias
                    cube = (v * v) * C1
                    t = jnp.tanh(v * (cube + C0))
                    double = (v * (1.0 + t)).astype(bf16)
                    act[there(b), cs] = double
                    t = t.astype(bf16)
                    slope = cube.astype(bf16) * bf16(3.0) + bf16(C0)
                    pre_grad[there(b), cs] = (bf16(1.0) + t) + double * ((bf16(1.0) - t) * slope)

        def output():
            out = nn(act[here, :], wb[...])
            sums = zero
            for b in blocks:
                r = out[local(b)] + (one[b, :] * g1 + (s1 + bb))
                c = r - row_mean(r)
                inv = lax.rsqrt(row_mean(c * c) + 1e-5)
                unit2 = c * inv
                last = min(b.stop, rows)
                lo_ref[0, b.start : last, :] = (unit2 * g2 + s2)[: last - b.start].astype(bf16)
                up = ct_ref[0, b.start : last, :].astype(f32)
                if last < b.stop:
                    up = jnp.concatenate([up, jnp.zeros((b.stop - last, width), f32)], 0)
                gu = up * g2
                back = inv * (gu - row_mean(gu) - unit2 * row_mean(gu * unit2))
                two[b, :] = back
                grad[there(b), :] = back.astype(bf16)
                sums = [a + fold(v) for a, v in zip(sums, (up * unit2, up, back))]
            for n in range(3):
                col[n] += sums[n]

        def hidden_grads():
            f = grad[here, :]
            for cs in chunks:
                da = nt(f, wb[cs, :])
                total = jnp.zeros((8, unit), f32)
                for b in blocks:
                    g = da[local(b)] * pre_grad[there(b), cs].astype(f32)
                    total = total + fold(g)
                    pre_grad[there(b), cs] = g.astype(bf16)
                binv[:, cs] += total

        def input_grads():
            out = nt(pre_grad[here, :], wi[...])
            sums = zero
            for b in blocks:
                dn = out[local(b)] + two[b, :]
                unit1 = one[b, :]
                gu = dn * g1
                back = inv1[b, 0:1] * (gu - row_mean(gu) - unit1 * row_mean(gu * unit1))
                gs_ref[0, b, :] = back
                ga_ref[0, b, :] = back.astype(bf16)
                sums = [a + fold(v) for a, v in zip(sums, (dn * unit1, dn, back))]
            for n in range(3):
                col[3 + n] += sums[n]

        return norm, hidden_units, output, hidden_grads, input_grads

    parts, tall = 2, 16
    size = pad // parts
    plan = [[(0, 0), (1, 0)], [(0, 1), (1, 1), (0, 2), (1, 2), (0, 3), (1, 3), (0, 4), (1, 4)]]
    sections = [chain(n * size, size, tall) for n in range(parts)]
    for at, group in enumerate(plan):

        @pl.when(step >= 0)
        def _():
            for p, n in group:
                sections[p][n]()

        if at == 0:

            @pl.when(step == 0)
            def _():
                for c in loads():
                    c.wait()
                wb[...] = wb[...] * bf16(0.5)

    ga = ga_ref[0]
    dot_ref[0, :, :pad] = nt(wo_ref[...], ga).astype(bf16)
    acc[...] += nn(mt_ref[0, :, :pad], ga)

    @pl.when(step == pl.num_programs(0) - 1)
    def _():
        n = width // planes
        size = n // INNER
        outs = (o0_ref, o1_ref)
        peers = [(half, hi) for half in range(2) for hi in range(INNER // 2)]
        for m, (at, cut) in enumerate(((0, cut_in), (cut_in, cut_back))):
            for s, cs in enumerate(chunks):
                piece = tn(low[...], pre_grad[:, cs]) if m == 0 else tn(act[:, cs], grad[...])
                turn[m] = piece.astype(bf16) if m == 0 else (0.5 * piece).astype(bf16)
                for half, hi in peers:
                    start = pl.multiple_of(slot_of(half, hi) * cut, cut)
                    outs[half][hi, s, at : at + cut, :] = turn[m, pl.ds(start, cut), :]
        at = cut_in + cut_back
        totals = jnp.sum(col[...], 1)
        bins = jnp.sum(binv[...], 0, keepdims=True)
        for s, cs in enumerate(chunks):
            plane = lax.rem(at_ref[1] + planes - s, planes)
            mine = jnp.zeros((8, n), f32)
            for p in range(planes):
                mine = jnp.where(plane == p, totals[:, n * p : n * p + n], mine)
            mine = jnp.concatenate([mine, jnp.zeros((8, width - n), f32)], 1)
            mine = jnp.where(lax.broadcasted_iota(jnp.int32, mine.shape, 0) == 6, bins[:, cs], mine)
            for half, hi in peers:
                slot = slot_of(half, hi)
                start = pl.multiple_of(plane * n + slot * size, size)
                outs[half][hi, s, at : at + size, :] = acc[pl.ds(start, size), :].astype(bf16)
                outs[half][hi, s, at + size :, :] = vector_rows(mine, slot, 16).astype(bf16)


def ffn(at, so, cotangent, mt, vec, wo, bi, bias_far, wi, wb, far):
    spans, pad, width = so.shape
    rows = cotangent.shape[1]
    own = wb.shape[0]
    planes = far[0].shape[0] + 1
    hidden = own * planes
    spec = lambda a, b: pl.BlockSpec((1, a, b), lambda i, *_: (i, 0, 0))
    st = lambda a, b, t: shape((spans, a, b), t)
    half = (INNER // 2, planes, (width + own) // INNER + width // (planes * INNER) + 16, width)
    out = pl.BlockSpec(half, lambda i, *_: (0, 0, 0, 0), pipeline_mode=pl.Buffered(1))
    total = spans * pad
    vmem = pltpu.VMEM
    return pl.pallas_call(
        functools.partial(ffn_body, rows, len(far), planes),
        grid_spec=pltpu.PrefetchScalarGridSpec(
            num_scalar_prefetch=1,
            grid=(spans,),
            in_specs=[spec(pad, width), spec(rows, width), spec(width, lanes(pad))] + [whole(w) for w in (vec, wo, bi, bias_far)]
            + [ANY] * (2 + len(far)),
            out_specs=[spec(rows, width), spec(pad, width), spec(pad, width), spec(width, lanes(pad)), out, out],
            scratch_shapes=[vmem((8, 8, width), f32), vmem((8, hidden), f32), vmem((width, hidden), bf16), vmem((hidden, width), bf16),
                            vmem((pad, width), f32), vmem((pad, width), f32), vmem((pad, 128), f32),
                            vmem((total, hidden), bf16), vmem((total, hidden), bf16), vmem((total, width), bf16),
                            vmem((total, width), bf16), vmem((width, width), f32), vmem((2, width, width), bf16),
                            pltpu.SemaphoreType.DMA((2 + 2 * len(far) * (planes - 1),))],
        ),
        out_shape=[st(rows, width, bf16), st(pad, width, f32), st(pad, width, bf16), st(width, lanes(pad), bf16)] + [shape(half, bf16)] * 2,
        compiler_params=params(62),
        cost_estimate=cost(46),
        name="ffn",
    )(at, so, cotangent, mt, vec, wo, bi, bias_far, wi, wb, *far)


def join_body(count, *refs):
    o_ref, b_ref = refs[-2:]
    rows = o_ref.shape[1]
    for i in range(count):
        o_ref[i] = refs[i][:rows, :]
        b_ref[i : i + 1, :] = refs[i][rows:, :].astype(f32)[0:1]


def join(parts, after):
    rows, width = parts[0].shape
    return pl.pallas_call(
        functools.partial(join_body, len(parts)),
        in_specs=[pl.BlockSpec(memory_space=pltpu.VMEM)] * len(parts) + [ANY] * len(after),
        out_specs=[pl.BlockSpec(memory_space=pltpu.VMEM)] * 2,
        out_shape=[shape((len(parts), rows - 16, width), bf16), shape((len(parts), width), f32)],
        compiler_params=params(),
        cost_estimate=cost(1),
        name="join",
    )(*parts, *after)


def add(*refs):
    total = refs[0][...].astype(f32)
    for ref in refs[1:]:
        total = total + ref[...].astype(f32)
    return total.astype(bf16)


def core_sum_body(pairs, axis, skip, *refs):
    outs = refs[2 * pairs + skip :]
    for p, o_ref in enumerate(outs):
        o_ref[...] = jnp.concatenate([add(refs[2 * i].at[p], refs[2 * i + 1].at[p]) for i in range(pairs)], axis)


def core_sum(pairs, axis, after, name):
    peers, planes, rows, width = pairs[0][0].shape
    if axis == 1:
        rows = sum(a.shape[2] for a, _ in pairs)
    else:
        width = sum(a.shape[3] for a, _ in pairs)
    flat = [a for pair in pairs for a in pair]
    return pl.pallas_call(
        functools.partial(core_sum_body, len(pairs), axis, len(after)),
        grid=(planes,),
        in_specs=[pl.BlockSpec((peers, 1) + a.shape[2:], lambda i: (0, i, 0, 0)) for a in flat] + [ANY] * len(after),
        out_specs=[pl.BlockSpec((1, rows, width), lambda i: (i, 0, 0))] * peers,
        out_shape=[shape((planes, rows, width), bf16)] * peers,
        compiler_params=params(),
        cost_estimate=cost(2),
        name=name,
    )(*flat, *after)


def plane_sum_body(count, skip, *refs):
    outs = refs[count + skip :]
    for s, o_ref in enumerate(outs):
        o_ref[...] = add(*(ref.at[s] for ref in refs[:count]))


def plane_sum(parts, after, name):
    planes, rows, width = parts[0].shape
    return pl.pallas_call(
        functools.partial(plane_sum_body, len(parts), len(after)),
        in_specs=[pl.BlockSpec(memory_space=pltpu.VMEM)] * len(parts) + [ANY] * len(after),
        out_specs=[pl.BlockSpec(memory_space=pltpu.VMEM)] * planes,
        out_shape=[shape((rows, width), bf16)] * planes,
        compiler_params=params(),
        cost_estimate=cost(2),
        name=name,
    )(*parts, *after)


def last_sum_body(count, groups, skip, *refs):
    o_ref = refs[count * groups + skip]
    at = 0
    for g in range(groups):
        part = add(*refs[count * g : count * g + count])
        o_ref[at : at + part.shape[0], :] = part
        at += part.shape[0]


def last_sum(groups, after, name):
    flat = [a for group in groups for a in group]
    rows = sum(group[0].shape[0] for group in groups)
    return pl.pallas_call(
        functools.partial(last_sum_body, len(groups[0]), len(groups), len(after)),
        in_specs=[pl.BlockSpec(memory_space=pltpu.VMEM)] * len(flat) + [ANY] * len(after),
        out_specs=pl.BlockSpec(memory_space=pltpu.VMEM),
        out_shape=shape((rows, flat[0].shape[1]), bf16),
        compiler_params=params(),
        cost_estimate=cost(2),
        name=name,
    )(*flat, *after)


def back_body(rows, planes, group, skip, at_ref, x_ref, qt_ref, k_ref, v_ref, mt_ref, dt_ref, lt_ref, *refs):
    dq_ref, dk_ref, dv_ref, o0_ref, o1_ref, aq, ak, av, ab, xp, vec, turn = refs[skip:]
    w, pad = k_ref.shape[2], k_ref.shape[1]
    width = x_ref.shape[-1]
    hs = width // HEADS
    scale = hs**-0.5
    main = rows // 128 * 128
    left = pad - main
    heads = w // hs
    top = rows // 16 * 16
    step = pl.program_id(0)

    @pl.when(step == 0)
    def _():
        aq[...] = jnp.zeros_like(aq)
        ak[...] = jnp.zeros_like(ak)
        av[...] = jnp.zeros_like(av)
        ab[...] = jnp.zeros_like(ab)
        xp[top:, :] = jnp.zeros((pad - top, width), bf16)

    xp[:rows, :] = x_ref[0]
    k = k_ref[0]
    kt = k.T
    v = v_ref[0]
    valid = lax.broadcasted_iota(jnp.int32, (pad - top, 1), 0) < rows - top

    def core(ks, qs, vs, ds, ls, ms):
        delta = jnp.sum(ds.astype(f32) * ms.astype(f32), 0, keepdims=True)
        st = nn(ks, qs)
        st = jnp.concatenate([st[:top], jnp.where(valid, st[top:], NEG)], 0)
        p = jnp.exp2(st - ls)
        gsc = (p * (nn(vs, ds) - delta)).astype(bf16)
        return p.astype(bf16), gsc

    same = (lax.broadcasted_iota(jnp.int32, (w, 128), 0) // hs
            == lax.broadcasted_iota(jnp.int32, (w, 128), 1) // left)
    tile = lambda a: jnp.where(same, jnp.concatenate([a] * heads, 1), 0).astype(bf16)
    ql, dl, ml = (tile(ref[0, :, main:pad]) for ref in (qt_ref, dt_ref, mt_ref))
    ll = jnp.concatenate([lt_ref[0, 0, h : h + 1, main:pad] for h in range(heads)], 1)
    p, gsc = core(k, ql, v, dl, ll, ml)
    dv_left = nt(dl, p)
    dk_left = nt(ql, gsc) * (1.0 / LOG2E)
    dq_left = nn(kt, gsc)
    for h in range(heads):
        c = slice(hs * h, hs * h + hs)
        q, d = qt_ref[0, c, :main], dt_ref[0, c, :main]
        p, gsc = core(k[:, c], q, v[:, c], d, lt_ref[0, 0, h : h + 1, :main], mt_ref[0, c, :main])
        dv_ref[0, c, :pad] = (nt(d, p) + dv_left[c]).astype(bf16)
        dk_ref[0, c, :pad] = (nt(q, gsc) * (1.0 / LOG2E) + dk_left[c]).astype(bf16)
        dq_ref[0, c, :main] = (nn(kt[c], gsc) * scale).astype(bf16)
        dq_ref[0, c, main:pad] = (dq_left[c, left * h : left * h + left] * scale).astype(bf16)
    x = xp[...]
    aq[...] += nn(dq_ref[0, :, :pad], x)
    ak[...] += nn(dk_ref[0, :, :pad], x)
    av[...] += nn(dv_ref[0, :, :pad], x)
    ab[:, 0:1] += jnp.sum(dq_ref[0, :, :pad].astype(f32), 1, keepdims=True)
    ab[:, 1:2] += jnp.sum(dv_ref[0, :, :pad].astype(f32), 1, keepdims=True)

    @pl.when(step == pl.num_programs(0) - 1)
    def _():
        size = width // (planes * INNER)
        n = width // planes
        vec[...] = jnp.zeros_like(vec)
        vec[:, group * w : group * w + w] = ab[...].T
        for i, a in enumerate((aq, ak, av)):
            turn[i] = a[...].T
        for half, o_ref in enumerate((o0_ref, o1_ref)):
            for hi in range(INNER // 2):
                for s in range(planes):
                    peer = half + 2 * hi
                    plane = lax.rem(at_ref[1] + planes - s, planes)
                    start = pl.multiple_of(plane * n + (at_ref[0] ^ peer) * size, size)
                    for i in range(3):
                        o_ref[hi, s, size * i : size * i + size, :] = turn[i, pl.ds(start, size), :].astype(bf16)
                    o_ref[hi, s, 3 * size :, :] = jnp.zeros((16, w), bf16)
                    mine = vec[:, pl.ds(pl.multiple_of(plane * n, n), n)]
                    o_ref[hi, s, 3 * size :, :n] = vector_rows(mine, at_ref[0] ^ peer, 16).astype(bf16)


def back(at, sequence, qt, k, v, mt, dt, lt, group, planes, after=()):
    spans, rows, width = sequence.shape
    pad = k.shape[1]
    wide = qt.shape[2]
    w = width // GROUPS
    tr = pl.BlockSpec((1, w, wide), lambda i, *_: (i, group, 0))
    nat = pl.BlockSpec((1, pad, w), lambda i, *_: (i, 0, group))
    grad = pl.BlockSpec((1, w, wide), lambda i, *_: (i, 0, 0))
    half = (INNER // 2, planes, 3 * width // (planes * INNER) + 16, w)
    out = pl.BlockSpec(half, lambda i, *_: (0, 0, 0, 0))
    return pl.pallas_call(
        functools.partial(back_body, rows, planes, group, len(after)),
        grid_spec=pltpu.PrefetchScalarGridSpec(
            num_scalar_prefetch=1,
            grid=(spans,),
            in_specs=[pl.BlockSpec((1, rows, width), lambda i, *_: (i, 0, 0)), tr,
                      nat, nat, tr, tr,
                      pl.BlockSpec((1, 1, HEADS // GROUPS, wide), lambda i, *_: (i, group, 0, 0))] + [ANY] * len(after),
            out_specs=[grad] * 3 + [out] * 2,
            scratch_shapes=[pltpu.VMEM((w, width), f32)] * 3
            + [pltpu.VMEM((w, 8), f32), pltpu.VMEM((pad, width), bf16), pltpu.VMEM((8, width), f32), pltpu.VMEM((3, width, w), f32)],
        ),
        out_shape=[shape((spans, w, wide), bf16)] * 3 + [shape(half, bf16)] * 2,
        compiler_params=params(),
        cost_estimate=cost(21),
        name=f"back{group}",
    )(at, sequence, qt, k, v, mt, dt, lt, *after)


def input_body(rows, groups, skip, *refs):
    refs = refs[skip:]
    gs_ref = refs[0]
    parts = refs[1 : 1 + 3 * groups]
    ws = refs[1 + 3 * groups : 4 + 3 * groups]
    out_ref = refs[4 + 3 * groups]
    wt = refs[5 + 3 * groups :]

    @pl.when(pl.program_id(0) == 0)
    def _():
        for a, b in zip(wt, ws):
            a[...] = b[...].T

    total = gs_ref[0]
    for g in range(groups):
        for n in range(3):
            part = parts[3 * g + n]
            w = part.shape[1]
            total = total + tn(part[0, :, : total.shape[0]], wt[n][w * g : w * g + w, :])
    out_ref[0] = total[:rows]


def input_grad(rows, gs, parts, wq, wk, wv, after=()):
    spans, pad, width = gs.shape
    flat = [a for part in parts for a in part]
    spec = lambda a: pl.BlockSpec((1,) + a.shape[1:], lambda i: (i, 0, 0))
    return pl.pallas_call(
        functools.partial(input_body, rows, len(parts), len(after)),
        grid=(spans,),
        in_specs=[ANY] * len(after) + [spec(gs)] + [spec(a) for a in flat] + [whole(w) for w in (wq, wk, wv)],
        out_specs=pl.BlockSpec((1, rows, width), lambda i: (i, 0, 0)),
        out_shape=shape((spans, rows, width), f32),
        scratch_shapes=[pltpu.VMEM((width, width), bf16)] * 3,
        compiler_params=params(),
        cost_estimate=cost(10),
        name="input_grad",
    )(*after, gs, *flat, wq, wk, wv)


def ffn_final_body(cut_in, cut_back, skip, at_ref, *refs):
    pieces = refs[:INNER]
    wi_ref, wb_ref, wo_ref, bin_ref, *vec_refs = refs[INNER + skip :]
    n, width = wo_ref.shape
    size = n // INNER
    for q in range(INNER):
        slot = at_ref[0] ^ (q // (INNER // 2) + 2 * (q % (INNER // 2)))
        p = pieces[q]
        wi_ref[pl.ds(pl.multiple_of(slot * cut_in, cut_in), cut_in), :] = p[:cut_in, :].astype(f32)
        at = cut_in
        wb_ref[pl.ds(pl.multiple_of(slot * cut_back, cut_back), cut_back), :] = p[at : at + cut_back, :].astype(f32)
        at += cut_back
        wo_ref[pl.ds(pl.multiple_of(slot * size, size), size), :] = p[at : at + size, :].astype(f32)
        tail = p[at + size :, :].astype(f32)[0:1]
        for i, v_ref in enumerate(vec_refs):

            @pl.when(slot == i)
            def _():
                v_ref[...] = tail[:, :n]

        @pl.when(slot == len(vec_refs))
        def _():
            bin_ref[...] = tail


def attend_final_body(skip, at_ref, *refs):
    pieces = refs[:INNER]
    wq_ref, wk_ref, wv_ref, *vec_refs = refs[INNER + skip :]
    n, width = wq_ref.shape
    size = n // INNER
    w = width // GROUPS
    for q in range(INNER):
        slot = at_ref[0] ^ (q // (INNER // 2) + 2 * (q % (INNER // 2)))
        p = pieces[q]
        for i, o_ref in enumerate((wq_ref, wk_ref, wv_ref)):
            o_ref[pl.ds(pl.multiple_of(slot * size, size), size), :] = p[size * i : size * i + size, :].astype(f32)
        tail = p[3 * size :, :].astype(f32)[0:1]
        pair = tail[:, :n]
        for g in range(1, GROUPS):
            pair = pair + tail[:, w * g : w * g + n]
        for i, v_ref in enumerate(vec_refs):

            @pl.when(slot == i)
            def _():
                v_ref[...] = pair


def final(body, at, pieces, out, after, name):
    return pl.pallas_call(
        functools.partial(body, len(after)),
        grid_spec=pltpu.PrefetchScalarGridSpec(
            num_scalar_prefetch=1,
            grid=(1,),
            in_specs=[whole(a) for a in pieces] + [ANY] * len(after),
            out_specs=[pl.BlockSpec(d, lambda *_: (0, 0)) for d in out],
        ),
        out_shape=[shape(d, f32) for d in out],
        compiler_params=params(),
        cost_estimate=cost(3),
        name=name,
    )(at, *pieces, *after)


def shards(dp, planes, sequence, cotangent, w_query, b_query, w_key, w_value, b_value, w_out, b_out, gain_attn, shift_attn,
           w_in, b_in, w_back, b_back, gain_ffn, shift_ffn):
    spans, rows, width = sequence.shape
    own = w_in.shape[1]
    at = jnp.stack([lax.axis_index("dp") & (INNER - 1), lax.axis_index("mp")]).astype(jnp.int32)

    def swap(a, k):
        return lax.ppermute(a, "dp", [(i, i ^ k) for i in range(dp)])

    def turn(a, s):
        return lax.ppermute(a, "mp", [(i, (i + s) % planes) for i in range(planes)])

    def spread(a, after=()):
        far = [a] + [swap(a, 2 * k) for k in range(1, INNER // 2)]
        far = lax.optimization_barrier((*far, *after))[: INNER // 2]
        return list(far) + [swap(b, 1) for b in far]

    def in_plane(parts, after, name):
        parts = [parts[0]] + [swap(parts[k], 2 * k) for k in range(1, INNER // 2)]
        totals = plane_sum(parts, after, name)
        step = INNER
        while step < dp:
            totals = [(t.astype(f32) + swap(t, step).astype(f32)).astype(bf16) for t in totals]
            step *= 2
        return totals

    def to_planes(totals):
        return [totals[0]] + [turn(totals[s], -s) for s in range(1, planes)]

    piece = prep(at, w_in, w_back, b_in)
    far = [turn(piece, s) for s in range(1, planes)]
    vec = stack_vectors((b_query, b_value, b_out, b_back, gain_attn, shift_attn, gain_ffn, shift_ffn), (piece,))
    common = (sequence, w_query, w_key, w_value, w_out, vec)
    head = 1
    first = attend(*common, 0, head)
    far, bias_far = join(far, first[:1])
    qt, k, v, mt, lt, so = attend(*common, head, spans - head, first, (far,))
    far = spread(far, (so,))
    layer_out, gs, ga, dt, keep, send = ffn(at, so, cotangent, mt, vec, w_out, b_in, bias_far, w_in, w_back, far)
    *grad0, keep0, send0 = back(at, sequence, qt, k, v, mt, dt, lt, 0, planes)
    ffn_parts = core_sum([(keep, swap(send, 1))], 1, (keep0,), "core_ffn")
    *grad1, keep1, send1 = back(at, sequence, qt, k, v, mt, dt, lt, 1, planes, (ffn_parts[0],))
    ffn_parts = to_planes(in_plane(ffn_parts, (keep1,), "plane_ffn"))
    parts = core_sum([(keep0, swap(send0, 1)), (keep1, swap(send1, 1))], 2, (ffn_parts[0],), "core_attn")
    by_input = input_grad(rows, gs, [grad0, grad1], w_query, w_key, w_value, (ffn_parts[0],))
    layer_out = lax.optimization_barrier(jnp.transpose(layer_out, (1, 0, 2)))
    totals = in_plane(parts, (by_input, layer_out), "plane_attn")
    ffn_sum = last_sum([ffn_parts], (totals[0],), "last_ffn")
    by_input = lax.optimization_barrier((by_input, ffn_sum))[0]
    by_input = lax.optimization_barrier(jnp.transpose(by_input, (1, 0, 2)))
    ffn_pieces = spread(ffn_sum)
    attn_sum = last_sum([to_planes(totals)], (ffn_sum, by_input), "last_attn")
    n = width // planes
    wi, wb, wo, bins, gg2, gs2, bb, gg1, gs1, bo = final(
        functools.partial(ffn_final_body, width // INNER, own // INNER), at, ffn_pieces,
        [(width, own), (own, width), (n, width), (1, own)] + [(1, n)] * 6, (attn_sum,), "ffn_final")
    attn_pieces = spread(attn_sum, (wi,))
    wq, wk, wv, bq, bv = final(attend_final_body, at, attn_pieces, [(n, width)] * 3 + [(1, n)] * 2, (), "attend_final")
    row = lambda a: a.reshape(-1)
    layer_out, by_input = (jnp.transpose(a, (1, 0, 2)) for a in (layer_out, by_input))
    return (layer_out, by_input, wq, row(bq), wk, wv, row(bv), wo, row(bo), row(gg1), row(gs1), wi, row(bins), wb,
            row(bb), row(gg2), row(gs2))


def solution(mesh):
    spans, vector = P(("dp", "mp"), None, None), P("mp")
    return jax.shard_map(
        functools.partial(shards, mesh.shape["dp"], mesh.shape["mp"]),
        mesh=mesh,
        in_specs=(spans, spans) + (P(),) * 9 + (P(None, "mp"), vector, P("mp", None)) + (P(),) * 3,
        out_specs=(spans, spans, P("mp", None), vector, P("mp", None), P("mp", None), vector, P("mp", None), vector, vector, vector,
                   P(None, "mp"), vector, P("mp", None), vector, vector, vector),
        check_vma=False,
    )
```

profile of v0, /device:TPU:0, one launch (start us, length us, event | category | flops | bytes accessed | tf_op | source)
XLA Modules:
  0.0 238.4 jit_solution(1163794510213393131)
XLA Ops:
  1.3 2.3 prep.1.refs_8_
  3.6 5.0 %collective-permute-start.2 = (bf16[144,512]{1,0:T(8,128)(2,1)}, bf16[144,512]{1,0:T(8,128)(2,1)S(1)}, u32[]{:S(2)}, u32[]{:S(2)}) collective-permute-start(bf16[144,512]{1,0:T(8,128)(2,1)} %prep.1.refs_8_), channel_id=1, source_target_pairs={{0,3},{1,0},{2,1},{3,2},{4,7},{5,4},{6,5},{7,6},{8,11},{9,8},{10,9... | collective-permute-start | bytes 442376 | tf_op jit(solution)/shard_map/ppermute | solution.py:718
  9.7 1.8 copy.41.x_ref
  12.9 7.3 %attend0.1 = (bf16[4,512,640]{2,1,0:T(8,128)(2,1)}, bf16[4,544,512]{2,1,0:T(8,128)(2,1)}, bf16[4,544,512]{2,1,0:T(8,128)(2,1)}, bf16[4,512,640]{2,1,0:T(8,128)(2...) custom-call(bf16[4,532,512]{2,1,0:T(8,128)(2,1)} %copy.41.x_ref, bf16[512,512]{1,0:T(8,128)(2,1)} %refs_8_.1, ...), custom_call_target="tpu_custom_call" | custom-call | flops 16000000000 | bytes 1600000 | tf_op jit(solution)/shard_map/attend0/pallas_call | solution.py:177
  22.0 1.8 join.1
  23.9 2.4 %collective-permute-start.5 = (bf16[3,128,512]{2,1,0:T(8,128)(2,1)}, bf16[3,128,512]{2,1,0:T(8,128)(2,1)S(1)}, u32[]{:S(2)}, u32[]{:S(2)}) collective-permute-start(bf16[3,128,512]{2,1,0:T(8,128)(2,1)} %get-tuple-element.100.refs_6_.refs_0_), channel_id=1, source_target_pairs={{0,24},{4,28},{8,16},{12,20},{16,8},{20,12},{24,0},{28,4},{1,25},{... | collective-permute-start | bytes 1179656 | tf_op jit(solution)/shard_map/ppermute | solution.py:715
  27.4 17.1 %attend1.1 = (bf16[4,512,640]{2,1,0:T(8,128)(2,1)}, bf16[4,544,512]{2,1,0:T(8,128)(2,1)}, bf16[4,544,512]{2,1,0:T(8,128)(2,1)}, bf16[4,512,640]{2,1,0:T(8,128)(2...) custom-call(bf16[4,532,512]{2,1,0:T(8,128)(2,1)} %copy.41.x_ref, ...), custom_call_target="tpu_custom_call", output_to_operand_aliasing={{0}: (6, {}), {1}: (7, {}), {2}: (8, {}), {3}: (9, {}), {4}... | custom-call | flops 16000000000 | bytes 1600000 | tf_op jit(solution)/shard_map/attend1/pallas_call | solution.py:177
  45.6 1.8 copy.42.ct_ref
  48.9 63.3 %ffn.1 = (bf16[4,532,512]{2,1,0:T(8,128)(2,1)}, f32[4,544,512]{2,1,0:T(8,128)}, bf16[4,544,512]{2,1,0:T(8,128)(2,1)}, bf16[4,512,640]{2,1,0:T(8,128)(2,1)}, bf16...) custom-call(s32[2]{0:T(128)} %pad_add_fusion.at_ref, f32[4,544,512]{2,1,0:T(8,128)} %get-tuple-element.97.so_ref, ...), custom_call_target="tpu_custom_call" | custom-call | flops 46000001024 | bytes 4600000 | tf_op jit(solution)/shard_map/ffn/pallas_call | solution.py:382
  112.3 21.0 %back0.1 = (bf16[4,256,640]{2,1,0:T(8,128)(2,1)}, bf16[4,256,640]{2,1,0:T(8,128)(2,1)}, bf16[4,256,640]{2,1,0:T(8,128)(2,1)}, bf16[4,4,64,256]{3,2,1,0:T(8,128)(2,1)}, bf16[4,4,64,256]{3,2,1,0:T(8,128)(2,1)}) custom-call(s32[2]{0:T(128)} %pad_add_fusion.at_ref, bf16[4,532,512]{2,1,0:T(8,128)(2,1)} %copy.41.x_ref, ...), custom_call_target="tpu_custom_call" | custom-call | flops 20999999488 | bytes 2100000 | tf_op jit(solution)/shard_map/back0/pallas_call | solution.py:587
  135.3 4.5 %core_ffn.1 = (bf16[4,160,512]{2,1,0:T(8,128)(2,1)}, bf16[4,160,512]{2,1,0:T(8,128)(2,1)}, bf16[4,160,512]{2,1,0:T(8,128)(2,1)}, bf16[4,160,512]{2,1,0:T(8,128)(2,1)}) custom-call(bf16[4,4,160,512]{3,2,1,0:T(8,128)(2,1)} %get-tuple-element.105.refs_0_, bf16[4,4,160,512]{3,2,1,0:T(8,128)(2,1)} %copy-done.6, ...), custom_call_target="tpu_custom_call" | custom-call | flops 2000000000 | bytes 200000 | tf_op jit(solution)/shard_map/core_ffn/pallas_call | solution.py:444
  143.3 21.1 %back1.1 = (bf16[4,256,640]{2,1,0:T(8,128)(2,1)}, bf16[4,256,640]{2,1,0:T(8,128)(2,1)}, bf16[4,256,640]{2,1,0:T(8,128)(2,1)}, bf16[4,4,64,256]{3,2,1,0:T(8,128)(2,1)}, bf16[4,4,64,256]{3,2,1,0:T(8,128)(2,1)}) custom-call(s32[2]{0:T(128)} %pad_add_fusion.at_ref, bf16[4,532,512]{2,1,0:T(8,128)(2,1)} %copy.41.x_ref, ...), custom_call_target="tpu_custom_call" | custom-call | flops 20999999488 | bytes 2100000 | tf_op jit(solution)/shard_map/back1/pallas_call | solution.py:587
  164.4 2.5 %copy.50 = bf16[4,532,512]{2,0,1:T(4,128)(2,1)} copy(bf16[4,532,512]{2,1,0:T(8,128)(2,1)S(1)} %copy-done) | data formatting | bytes 4358144 | tf_op jit(solution)/shard_map/ffn/pallas_call | solution.py:382
  166.9 5.1 %collective-permute-done.12.refs_2_ = bf16[4,160,512]{2,1,0:T(8,128)(2,1)S(1)} collective-permute-done((bf16[4,160,512]{2,1,0:T(8,128)(2,1)}, bf16[4,160,512]{2,1,0:T(8,128)(2,1)S(1)}, u32[]{:S(2)}, u32[]{:S(2)}) %collective-permute-start.12) | collective-permute-done | bytes 655392 | tf_op jit(solution)/shard_map/ppermute | solution.py:715
  172.8 2.7 %plane_ffn.1 = (bf16[160,512]{1,0:T(8,128)(2,1)}, bf16[160,512]{1,0:T(8,128)(2,1)}, bf16[160,512]{1,0:T(8,128)(2,1)}, bf16[160,512]{1,0:T(8,128)(2,1)}) custom-call(bf16[4,160,512]{2,1,0:T(8,128)(2,1)} %get-tuple-element.113.refs_0_, bf16[4,160,512]{2,1,0:T(8,128)(2,1)} %copy-done.7, bf16[4,160,512]{2,1,0:T(8,128)(2,1)} %copy-done.8, ...), custom_call_target="tpu_custom_call" | custom-call | flops 2000000000 | bytes 200000 | tf_op jit(solution)/shard_map/plane_ffn/pallas_call | solution.py:464
  179.2 3.8 %core_attn.1 = (bf16[4,64,512]{2,1,0:T(8,128)(2,1)}, bf16[4,64,512]{2,1,0:T(8,128)(2,1)}, bf16[4,64,512]{2,1,0:T(8,128)(2,1)}, bf16[4,64,512]{2,1,0:T(8,128)(2,1)}) custom-call(bf16[4,4,64,256]{3,2,1,0:T(8,128)(2,1)} %get-tuple-element.112.refs_2_.refs_0_, bf16[4,4,64,256]{3,2,1,0:T(8,128)(2,1)} %copy-done.9, ...), custom_call_target="tpu_custom_call" | custom-call | flops 2000000000 | bytes 200000 | tf_op jit(solution)/shard_map/core_attn/pallas_call | solution.py:444
  186.5 9.9 %input_grad.1.refs_4_ = f32[4,532,512]{2,1,0:T(8,128)} custom-call(bf16[160,512]{1,0:T(8,128)(2,1)} %get-tuple-element.118.refs_0_.refs_4_, f32[4,544,512]{2,1,0:T(8,128)} %get-tuple-element.119.refs_1_, bf16[4,256,640]{2,1,0:T(8,128)(2,1)} %get-tuple-element.120.refs_2_, bf16[4,256,640]{2,1,0:T(8,128)(2,1)} %get-tuple-element.121.refs_3_, ...), custom_call_target="tpu_custom_call" | custom-call | flops 10000000000 | bytes 1000000 | tf_op jit(solution)/shard_map/input_grad/pallas_call | solution.py:632
  196.4 1.9 collective-permute-start.16
  199.2 1.9 plane_attn.1
  201.1 2.5 %collective-permute-done.16.refs_3_ = bf16[160,512]{1,0:T(8,128)(2,1)S(1)} collective-permute-done((bf16[160,512]{1,0:T(8,128)(2,1)S(1)}, bf16[160,512]{1,0:T(8,128)(2,1)S(1)}, u32[]{:S(2)}, u32[]{:S(2)}) %collective-permute-start.16) | collective-permute-done | bytes 163872 | tf_op jit(solution)/shard_map/ppermute | solution.py:718
  204.3 1.9 last_ffn.1.refs_4_.refs_0_
  212.8 7.2 %copy.49 = f32[4,532,512]{2,0,1:T(4,128)} copy(f32[4,532,512]{2,1,0:T(8,128)} %input_grad.1.refs_4_) | data formatting | bytes 8716288 | tf_op jit(solution)/shard_map/optimization_barrier | solution.py:756
  228.4 3.9 %ffn_final.1 = (f32[512,512]{1,0:T(8,128)}, f32[512,512]{1,0:T(8,128)}, f32[128,512]{1,0:T(8,128)}, f32[1,512]{1,0:T(1,128)}, f32[1,128]{1,0:T(1,128)}, /*index=...) custom-call(s32[2]{0:T(128)} %pad_add_fusion.at_ref, ...), custom_call_target="tpu_custom_call" | custom-call | flops 3000000000 | bytes 300000 | tf_op jit(solution)/shard_map/ffn_final/pallas_call | solution.py:693
  235.5 2.7 %attend_final.1 = (f32[128,512]{1,0:T(8,128)}, f32[128,512]{1,0:T(8,128)}, f32[128,512]{1,0:T(8,128)}, f32[1,128]{1,0:T(1,128)}, f32[1,128]{1,0:T(1,128)}) custom-call(s32[2]{0:T(128)} %pad_add_fusion.at_ref, bf16[64,512]{1,0:T(8,128)(2,1)} %last_attn.1.refs_8_.refs_0_, bf16[64,512]{1,0:T(8,128)(2,1)} %copy-done.38, bf16[64,512]{1,0:T(8,128)(2,1)} %copy-done.36, ...), custom_call_target="tpu_custom_call" | custom-call | flops 3000000000 | bytes 300000 | tf_op jit(solution)/shard_map/attend_final/pallas_call | solution.py:693
  (170 shorter events, 41.8 us)
Async XLA Ops:
  3.6 16.6 %collective-permute-start.2 = (bf16[144,512]{1,0:T(8,128)(2,1)}, bf16[144,512]{1,0:T(8,128)(2,1)S(1)}, u32[]{:S(2)}, u32[]{:S(2)}) collective-permute-start(bf16[144,512]{1,0:T(8,128)(2,1)} %prep.1.refs_8_), channel_id=1, source_target_pairs={{0,3},{1,0},{2,1},{3,2},{4,7},{5,4},{6,5},{7,6},{8,11},{9,8},{10,9... | collective-permute-start | bytes 442376 | tf_op jit(solution)/shard_map/ppermute | solution.py:718
  8.6 12.7 %collective-permute-start.1 = (bf16[144,512]{1,0:T(8,128)(2,1)}, bf16[144,512]{1,0:T(8,128)(2,1)S(1)}, u32[]{:S(2)}, u32[]{:S(2)}) collective-permute-start(bf16[144,512]{1,0:T(8,128)(2,1)} %prep.1.refs_8_), channel_id=1, source_target_pairs={{0,2},{1,3},{2,0},{3,1},{4,6},{5,7},{6,4},{7,5},{8,10},{9,11},{10,... | collective-permute-start | bytes 442376 | tf_op jit(solution)/shard_map/ppermute | solution.py:718
  8.6 12.7 %collective-permute-start = (bf16[144,512]{1,0:T(8,128)(2,1)}, bf16[144,512]{1,0:T(8,128)(2,1)S(1)}, u32[]{:S(2)}, u32[]{:S(2)}) collective-permute-start(bf16[144,512]{1,0:T(8,128)(2,1)} %prep.1.refs_8_), channel_id=1, source_target_pairs={{0,1},{1,2},{2,3},{3,0},{4,5},{5,6},{6,7},{7,4},{8,9},{9,10},{10,1... | collective-permute-start | bytes 442376 | tf_op jit(solution)/shard_map/ppermute | solution.py:718
  23.9 20.6 %collective-permute-start.5 = (bf16[3,128,512]{2,1,0:T(8,128)(2,1)}, bf16[3,128,512]{2,1,0:T(8,128)(2,1)S(1)}, u32[]{:S(2)}, u32[]{:S(2)}) collective-permute-start(bf16[3,128,512]{2,1,0:T(8,128)(2,1)} %get-tuple-element.100.refs_6_.refs_0_), channel_id=1, source_target_pairs={{0,24},{4,28},{8,16},{12,20},{16,8},{20,12},{24,0},{28,4},{1,25},{... | collective-permute-start | bytes 1179656 | tf_op jit(solution)/shard_map/ppermute | solution.py:715
  26.3 18.1 %collective-permute-start.4 = (bf16[3,128,512]{2,1,0:T(8,128)(2,1)}, bf16[3,128,512]{2,1,0:T(8,128)(2,1)S(1)}, u32[]{:S(2)}, u32[]{:S(2)}) collective-permute-start(bf16[3,128,512]{2,1,0:T(8,128)(2,1)} %get-tuple-element.100.refs_6_.refs_0_), channel_id=1, source_target_pairs={{0,16},{4,20},{8,24},{12,28},{16,0},{20,4},{24,8},{28,12},{1,17},{... | collective-permute-start | bytes 1179656 | tf_op jit(solution)/shard_map/ppermute | solution.py:715
  26.8 17.6 %collective-permute-start.3 = (bf16[3,128,512]{2,1,0:T(8,128)(2,1)}, bf16[3,128,512]{2,1,0:T(8,128)(2,1)S(1)}, u32[]{:S(2)}, u32[]{:S(2)}) collective-permute-start(bf16[3,128,512]{2,1,0:T(8,128)(2,1)} %get-tuple-element.100.refs_6_.refs_0_), channel_id=1, source_target_pairs={{0,8},{4,12},{8,0},{12,4},{16,24},{20,28},{24,16},{28,20},{1,9},{5... | collective-permute-start | bytes 1179656 | tf_op jit(solution)/shard_map/ppermute | solution.py:715
  112.2 21.6 %collective-permute-start.10 = (bf16[4,4,160,512]{3,2,1,0:T(8,128)(2,1)}, bf16[4,4,160,512]{3,2,1,0:T(8,128)(2,1)S(1)}, u32[]{:S(2)}, u32[]{:S(2)}) collective-permute-start(bf16[4,4,160,512]{3,2,1,0:T(8,128)(2,1)} %get-tuple-element.106), channel_id=1, source_target_pairs={{0,4},{4,0},{8,12},{12,8},{16,20},{20,16},{24,28},{28,24},{1,5},{5... | collective-permute-start | bytes 7864328 | tf_op jit(solution)/shard_map/ppermute | solution.py:715
  133.3 45.1 %collective-permute-start.17 = (bf16[4,4,64,256]{3,2,1,0:T(8,128)(2,1)}, bf16[4,4,64,256]{3,2,1,0:T(8,128)(2,1)S(1)}, u32[]{:S(2)}, u32[]{:S(2)}) collective-permute-start(bf16[4,4,64,256]{3,2,1,0:T(8,128)(2,1)} %get-tuple-element.129), channel_id=1, source_target_pairs={{0,4},{4,0},{8,12},{12,8},{16,20},{20,16},{24,28},{28,24},{1,5},{5... | collective-permute-start | bytes 1572872 | tf_op jit(solution)/shard_map/ppermute | solution.py:715
  139.8 27.1 %collective-permute-start.11 = (bf16[4,160,512]{2,1,0:T(8,128)(2,1)}, bf16[4,160,512]{2,1,0:T(8,128)(2,1)S(1)}, u32[]{:S(2)}, u32[]{:S(2)}) collective-permute-start(bf16[4,160,512]{2,1,0:T(8,128)(2,1)} %get-tuple-element.114), channel_id=1, source_target_pairs={{0,8},{4,12},{8,0},{12,4},{16,24},{20,28},{24,16},{28,20},{1,9},{5... | collective-permute-start | bytes 1966088 | tf_op jit(solution)/shard_map/ppermute | solution.py:715
  141.3 30.7 %collective-permute-start.12 = (bf16[4,160,512]{2,1,0:T(8,128)(2,1)}, bf16[4,160,512]{2,1,0:T(8,128)(2,1)S(1)}, u32[]{:S(2)}, u32[]{:S(2)}) collective-permute-start(bf16[4,160,512]{2,1,0:T(8,128)(2,1)} %get-tuple-element.115), channel_id=1, source_target_pairs={{0,16},{4,20},{8,24},{12,28},{16,0},{20,4},{24,8},{28,12},{1,17},{... | collective-permute-start | bytes 1966088 | tf_op jit(solution)/shard_map/ppermute | solution.py:715
  142.8 29.2 %collective-permute-start.13 = (bf16[4,160,512]{2,1,0:T(8,128)(2,1)}, bf16[4,160,512]{2,1,0:T(8,128)(2,1)}, u32[]{:S(2)}, u32[]{:S(2)}) collective-permute-start(bf16[4,160,512]{2,1,0:T(8,128)(2,1)} %get-tuple-element.116), channel_id=1, source_target_pairs={{0,24},{4,28},{8,16},{12,20},{16,8},{20,12},{24,0},{28,4},{1,25},{... | collective-permute-start | bytes 1966088 | tf_op jit(solution)/shard_map/ppermute | solution.py:715
  164.3 14.0 %collective-permute-start.18 = (bf16[4,4,64,256]{3,2,1,0:T(8,128)(2,1)}, bf16[4,4,64,256]{3,2,1,0:T(8,128)(2,1)}, u32[]{:S(2)}, u32[]{:S(2)}) collective-permute-start(bf16[4,4,64,256]{3,2,1,0:T(8,128)(2,1)} %get-tuple-element.130), channel_id=1, source_target_pairs={{0,4},{4,0},{8,12},{12,8},{16,20},{20,16},{24,28},{28,24},{1,5},{5... | collective-permute-start | bytes 1572872 | tf_op jit(solution)/shard_map/ppermute | solution.py:715
  175.5 25.6 %collective-permute-start.14 = (bf16[160,512]{1,0:T(8,128)(2,1)}, bf16[160,512]{1,0:T(8,128)(2,1)S(1)}, u32[]{:S(2)}, u32[]{:S(2)}) collective-permute-start(bf16[160,512]{1,0:T(8,128)(2,1)} %get-tuple-element.126), channel_id=1, source_target_pairs={{0,3},{1,0},{2,1},{3,2},{4,7},{5,4},{6,5},{7,6},{8,11},{9,8},{10,9... | collective-permute-start | bytes 491528 | tf_op jit(solution)/shard_map/ppermute | solution.py:718
  177.2 23.9 %collective-permute-start.15 = (bf16[160,512]{1,0:T(8,128)(2,1)}, bf16[160,512]{1,0:T(8,128)(2,1)S(1)}, u32[]{:S(2)}, u32[]{:S(2)}) collective-permute-start(bf16[160,512]{1,0:T(8,128)(2,1)} %get-tuple-element.127), channel_id=1, source_target_pairs={{0,2},{1,3},{2,0},{3,1},{4,6},{5,7},{6,4},{7,5},{8,10},{9,11},{10,... | collective-permute-start | bytes 491528 | tf_op jit(solution)/shard_map/ppermute | solution.py:718
  183.0 13.4 %collective-permute-start.19 = (bf16[4,64,512]{2,1,0:T(8,128)(2,1)}, bf16[4,64,512]{2,1,0:T(8,128)(2,1)S(1)}, u32[]{:S(2)}, u32[]{:S(2)}) collective-permute-start(bf16[4,64,512]{2,1,0:T(8,128)(2,1)} %get-tuple-element.132), channel_id=1, source_target_pairs={{0,8},{4,12},{8,0},{12,4},{16,24},{20,28},{24,16},{28,20},{1,9},{5... | collective-permute-start | bytes 786440 | tf_op jit(solution)/shard_map/ppermute | solution.py:715
  183.5 14.9 %collective-permute-start.20 = (bf16[4,64,512]{2,1,0:T(8,128)(2,1)}, bf16[4,64,512]{2,1,0:T(8,128)(2,1)S(1)}, u32[]{:S(2)}, u32[]{:S(2)}) collective-permute-start(bf16[4,64,512]{2,1,0:T(8,128)(2,1)} %get-tuple-element.133), channel_id=1, source_target_pairs={{0,16},{4,20},{8,24},{12,28},{16,0},{20,4},{24,8},{28,12},{1,17},{... | collective-permute-start | bytes 786440 | tf_op jit(solution)/shard_map/ppermute | solution.py:715
  185.0 13.3 %collective-permute-start.21 = (bf16[4,64,512]{2,1,0:T(8,128)(2,1)}, bf16[4,64,512]{2,1,0:T(8,128)(2,1)S(1)}, u32[]{:S(2)}, u32[]{:S(2)}) collective-permute-start(bf16[4,64,512]{2,1,0:T(8,128)(2,1)} %get-tuple-element.134), channel_id=1, source_target_pairs={{0,24},{4,28},{8,16},{12,20},{16,8},{20,12},{24,0},{28,4},{1,25},{... | collective-permute-start | bytes 786440 | tf_op jit(solution)/shard_map/ppermute | solution.py:715
  207.7 12.3 %collective-permute-start.29 = (bf16[160,512]{1,0:T(8,128)(2,1)}, bf16[160,512]{1,0:T(8,128)(2,1)S(1)}, u32[]{:S(2)}, u32[]{:S(2)}) collective-permute-start(bf16[160,512]{1,0:T(8,128)(2,1)} %last_ffn.1.refs_4_.refs_0_), channel_id=1, source_target_pairs={{0,16},{4,20},{8,24},{12,28},{16,0},{20,4},{24,8},{28,12},{1,17},{... | collective-permute-start | bytes 491528 | tf_op jit(solution)/shard_map/ppermute | solution.py:715
  208.2 11.8 %collective-permute-start.28 = (bf16[160,512]{1,0:T(8,128)(2,1)}, bf16[160,512]{1,0:T(8,128)(2,1)S(1)}, u32[]{:S(2)}, u32[]{:S(2)}) collective-permute-start(bf16[160,512]{1,0:T(8,128)(2,1)} %last_ffn.1.refs_4_.refs_0_), channel_id=1, source_target_pairs={{0,8},{4,12},{8,0},{12,4},{16,24},{20,28},{24,16},{28,20},{1,9},{5... | collective-permute-start | bytes 491528 | tf_op jit(solution)/shard_map/ppermute | solution.py:715
  209.7 10.9 %collective-permute-start.22 = (bf16[64,512]{1,0:T(8,128)(2,1)S(1)}, bf16[64,512]{1,0:T(8,128)(2,1)S(1)}, u32[]{:S(2)}, u32[]{:S(2)}) collective-permute-start(bf16[64,512]{1,0:T(8,128)(2,1)S(1)} %copy-done.39), channel_id=1, source_target_pairs={{0,3},{1,0},{2,1},{3,2},{4,7},{5,4},{6,5},{7,6},{8,11},{9,8},{10,9... | collective-permute-start | bytes 196616 | tf_op jit(solution)/shard_map/ppermute | solution.py:718
  209.7 11.0 %collective-permute-start.23 = (bf16[64,512]{1,0:T(8,128)(2,1)S(1)}, bf16[64,512]{1,0:T(8,128)(2,1)S(1)}, u32[]{:S(2)}, u32[]{:S(2)}) collective-permute-start(bf16[64,512]{1,0:T(8,128)(2,1)S(1)} %copy-done.37), channel_id=1, source_target_pairs={{0,2},{1,3},{2,0},{3,1},{4,6},{5,7},{6,4},{7,5},{8,10},{9,11},{10,... | collective-permute-start | bytes 196616 | tf_op jit(solution)/shard_map/ppermute | solution.py:718
  212.7 8.4 %collective-permute-start.24 = (bf16[64,512]{1,0:T(8,128)(2,1)S(1)}, bf16[64,512]{1,0:T(8,128)(2,1)S(1)}, u32[]{:S(2)}, u32[]{:S(2)}) collective-permute-start(bf16[64,512]{1,0:T(8,128)(2,1)S(1)} %copy-done.35), channel_id=1, source_target_pairs={{0,1},{1,2},{2,3},{3,0},{4,5},{5,6},{6,7},{7,4},{8,9},{9,10},{10,1... | collective-permute-start | bytes 196616 | tf_op jit(solution)/shard_map/ppermute | solution.py:718
  223.5 8.8 %collective-permute-start.27 = (bf16[64,512]{1,0:T(8,128)(2,1)}, bf16[64,512]{1,0:T(8,128)(2,1)S(1)}, u32[]{:S(2)}, u32[]{:S(2)}) collective-permute-start(bf16[64,512]{1,0:T(8,128)(2,1)} %last_attn.1.refs_8_.refs_0_), channel_id=1, source_target_pairs={{0,24},{4,28},{8,16},{12,20},{16,8},{20,12},{24,0},{28,4},{1,25},{... | collective-permute-start | bytes 196616 | tf_op jit(solution)/shard_map/ppermute | solution.py:715
  225.1 7.3 %collective-permute-start.26 = (bf16[64,512]{1,0:T(8,128)(2,1)}, bf16[64,512]{1,0:T(8,128)(2,1)S(1)}, u32[]{:S(2)}, u32[]{:S(2)}) collective-permute-start(bf16[64,512]{1,0:T(8,128)(2,1)} %last_attn.1.refs_8_.refs_0_), channel_id=1, source_target_pairs={{0,16},{4,20},{8,24},{12,28},{16,0},{20,4},{24,8},{28,12},{1,17},{... | collective-permute-start | bytes 196616 | tf_op jit(solution)/shard_map/ppermute | solution.py:715
  (62 other events, 237.6 us)
where the time goes:
time: 243 us; the launch traced here: 238 us
  Pallas kernels  168 us (69%)
  starting transfers between devices  34.1 us (14%)
  local copies, waits for them, and re-layouts  22.6 us (9%)
  waiting for transfers between devices  11.7 us (5%)
    pallas_call x1, Pallas kernels, ffn(): pl.pallas_call(functools.partial(ffn_body, rows, len(far), planes), grid_...  63.3 us
    pallas_call x2, Pallas kernels, back(): pl.pallas_call(functools.partial(back_body, rows, planes, group, len(afte...  42 us
    pallas_call x2, Pallas kernels, attend(): pl.pallas_call(functools.partial(attend_body, rows, pad, len(before) + le...  24.4 us
    ppermute x30, starting transfers between devices, swap(): return lax.ppermute(a, 'dp', [(i, i ^ k) for i in range(dp)])  21.5 us
    unnamed x96, local copies, waits for them, and re-layouts  13 us
    ppermute x9, starting transfers between devices, turn(): return lax.ppermute(a, 'mp', [(i, (i + s) % planes) for i in range(planes)])  12.5 us
    pallas_call x1, Pallas kernels, input_grad(): pl.pallas_call(functools.partial(input_body, rows, len(parts), len(after)...  9.9 us
    pallas_call x2, Pallas kernels, core_sum(): pl.pallas_call(functools.partial(core_sum_body, len(pairs), axis, len(aft...  8.31 us
  transfers between devices with their start and end apart: 39, of which 9 were waited for; matrix products, arithmetic and copies ran while one was open for 6% of the time, Pallas kernels for 40%

commit v1 on v0

--- a/solution.py
+++ b/solution.py
@@ -108,7 +108,7 @@
 
 
 def attend_body(rows, pad, skip, x_ref, wq_ref, wk_ref, wv_ref, wo_ref, vec_ref, *refs):
-    qt_ref, k_ref, v_ref, mt_ref, lt_ref, so_ref, xp, vt = refs[skip:]
+    qt_ref, k_ref, v_ref, mt_ref, lt_ref, so_ref, q_ref, xp, vt = refs[skip:]
     width = x_ref.shape[-1]
     hs = width // HEADS
     main = rows // 128 * 128
@@ -123,7 +123,9 @@
     xp[:rows, :] = x_ref[0]
     x = xp[...]
     scale = hs**-0.5
-    qt_ref[0, :, :pad] = ((nn(x, wq_ref[...]) + vec_ref[0:1, :]) * (scale * LOG2E)).astype(bf16).T
+    q = ((nn(x, wq_ref[...]) + vec_ref[0:1, :]) * (scale * LOG2E)).astype(bf16)
+    q_ref[0] = q
+    qt_ref[0, :, :pad] = q.T
     k_ref[0] = nn(x, wk_ref[...]).astype(bf16)
     v = (nn(x, wv_ref[...]) + vec_ref[1:2, :]).astype(bf16)
     v_ref[0] = v
@@ -179,9 +181,10 @@
         grid=(count,),
         in_specs=[spec(rows, width)] + [whole(w) for w in (wq, wk, wv, wo, vec)] + [ANY] * (len(before) + len(after)),
         out_specs=[spec(width, wide), spec(pad, width), spec(pad, width), spec(width, wide),
-                   pl.BlockSpec((1, GROUPS, per, wide), lambda i: (i + first, 0, 0, 0)), spec(pad, width)],
+                   pl.BlockSpec((1, GROUPS, per, wide), lambda i: (i + first, 0, 0, 0)), spec(pad, width), spec(pad, width)],
         out_shape=[shape((spans, width, wide), bf16), shape((spans, pad, width), bf16), shape((spans, pad, width), bf16),
-                   shape((spans, width, wide), bf16), shape((spans, GROUPS, per, wide), f32), shape((spans, pad, width), f32)],
+                   shape((spans, width, wide), bf16), shape((spans, GROUPS, per, wide), f32), shape((spans, pad, width), f32),
+                   shape((spans, pad, width), bf16)],
         scratch_shapes=[pltpu.VMEM((pad, width), bf16), pltpu.VMEM((width, pad), bf16)],
         input_output_aliases={6 + n: n for n in range(len(before))},
         compiler_params=params(),
@@ -197,8 +200,8 @@
 
 
 def ffn_body(rows, slices, planes, at_ref, so_ref, ct_ref, mt_ref, vec_ref, wo_ref, bi_ref, bf_ref, wi_ref, wb_ref, *refs):
-    (lo_ref, gs_ref, ga_ref, dot_ref, o0_ref, o1_ref,
-     col, binv, wi, wb, one, two, inv1, act, pre_grad, low, grad, acc, turn, sem) = refs[slices:]
+    (lo_ref, gs_ref, d_ref, dot_ref, o0_ref, o1_ref,
+     col, binv, wi, wb, one, two, inv1, act, pre_grad, low, grad, acc, turn, low_grad, sem) = refs[slices:]
     pad, width = so_ref.shape[1:]
     own = wb_ref.shape[0]
     hidden = wb.shape[0]
@@ -257,13 +260,12 @@
             for cs, add_bias in zip(chunks, bias):
                 pre = nn(nl, wi[:, cs])
                 for b in blocks:
-                    v = pre[local(b)] + add_bias
-                    cube = (v * v) * C1
-                    t = jnp.tanh(v * (cube + C0))
-                    double = (v * (1.0 + t)).astype(bf16)
+                    v = (pre[local(b)] + add_bias).astype(bf16)
+                    cube = (v * v) * bf16(C1)
+                    t = jnp.tanh(v * (cube + bf16(C0)))
+                    double = v * (bf16(1.0) + t)
                     act[there(b), cs] = double
-                    t = t.astype(bf16)
-                    slope = cube.astype(bf16) * bf16(3.0) + bf16(C0)
+                    slope = cube * bf16(3.0) + bf16(C0)
                     pre_grad[there(b), cs] = (bf16(1.0) + t) + double * ((bf16(1.0) - t) * slope)
 
         def output():
@@ -307,7 +309,7 @@
                 gu = dn * g1
                 back = inv1[b, 0:1] * (gu - row_mean(gu) - unit1 * row_mean(gu * unit1))
                 gs_ref[0, b, :] = back
-                ga_ref[0, b, :] = back.astype(bf16)
+                low_grad[b, :] = back.astype(bf16)
                 sums = [a + fold(v) for a, v in zip(sums, (dn * unit1, dn, back))]
             for n in range(3):
                 col[3 + n] += sums[n]
@@ -333,8 +335,10 @@
                     c.wait()
                 wb[...] = wb[...] * bf16(0.5)
 
-    ga = ga_ref[0]
-    dot_ref[0, :, :pad] = nt(wo_ref[...], ga).astype(bf16)
+    ga = low_grad[...]
+    d = nt(ga, wo_ref[...]).astype(bf16)
+    d_ref[0] = d
+    dot_ref[0, :, :pad] = d.T
     acc[...] += nn(mt_ref[0, :, :pad], ga)
 
     @pl.when(step == pl.num_programs(0) - 1)
@@ -391,6 +395,7 @@
                             vmem((pad, width), f32), vmem((pad, width), f32), vmem((pad, 128), f32),
                             vmem((total, hidden), bf16), vmem((total, hidden), bf16), vmem((total, width), bf16),
                             vmem((total, width), bf16), vmem((width, width), f32), vmem((2, width, width), bf16),
+                            vmem((pad, width), bf16),
                             pltpu.SemaphoreType.DMA((2 + 2 * len(far) * (planes - 1),))],
         ),
         out_shape=[st(rows, width, bf16), st(pad, width, f32), st(pad, width, bf16), st(width, lanes(pad), bf16)] + [shape(half, bf16)] * 2,
@@ -428,27 +433,24 @@
     return total.astype(bf16)
 
 
-def core_sum_body(pairs, axis, skip, *refs):
+def core_sum_body(pairs, skip, *refs):
     outs = refs[2 * pairs + skip :]
     for p, o_ref in enumerate(outs):
-        o_ref[...] = jnp.concatenate([add(refs[2 * i].at[p], refs[2 * i + 1].at[p]) for i in range(pairs)], axis)
-
-
-def core_sum(pairs, axis, after, name):
-    peers, planes, rows, width = pairs[0][0].shape
-    if axis == 1:
-        rows = sum(a.shape[2] for a, _ in pairs)
-    else:
-        width = sum(a.shape[3] for a, _ in pairs)
+        o_ref[...] = jnp.concatenate([add(refs[2 * i].at[p], refs[2 * i + 1].at[p]) for i in range(pairs)], 1)
+
+
+def core_sum(pairs, after, name):
+    peers, planes, _, width = pairs[0][0].shape
+    rows = sum(a.shape[2] for a, _ in pairs)
     flat = [a for pair in pairs for a in pair]
     return pl.pallas_call(
-        functools.partial(core_sum_body, len(pairs), axis, len(after)),
+        functools.partial(core_sum_body, len(pairs), len(after)),
         grid=(planes,),
         in_specs=[pl.BlockSpec((peers, 1) + a.shape[2:], lambda i: (0, i, 0, 0)) for a in flat] + [ANY] * len(after),
         out_specs=[pl.BlockSpec((1, rows, width), lambda i: (i, 0, 0))] * peers,
         out_shape=[shape((planes, rows, width), bf16)] * peers,
         compiler_params=params(),
-        cost_estimate=cost(2),
+        cost_estimate=cost(0.001),
         name=name,
     )(*flat, *after)
 
@@ -467,7 +469,7 @@
         out_specs=[pl.BlockSpec(memory_space=pltpu.VMEM)] * planes,
         out_shape=[shape((rows, width), bf16)] * planes,
         compiler_params=params(),
-        cost_estimate=cost(2),
+        cost_estimate=cost(0.001),
         name=name,
     )(*parts, *after)
 
@@ -476,9 +478,9 @@
     o_ref = refs[count * groups + skip]
     at = 0
     for g in range(groups):
-        part = add(*refs[count * g : count * g + count])
-        o_ref[at : at + part.shape[0], :] = part
-        at += part.shape[0]
+        total = add(*refs[count * g : count * g + count])
+        o_ref[at : at + total.shape[0], :] = total
+        at += total.shape[0]
 
 
 def last_sum(groups, after, name):
@@ -490,13 +492,13 @@
         out_specs=pl.BlockSpec(memory_space=pltpu.VMEM),
         out_shape=shape((rows, flat[0].shape[1]), bf16),
         compiler_params=params(),
-        cost_estimate=cost(2),
+        cost_estimate=cost(0.001),
         name=name,
     )(*flat, *after)
 
 
-def back_body(rows, planes, group, skip, at_ref, x_ref, qt_ref, k_ref, v_ref, mt_ref, dt_ref, lt_ref, *refs):
-    dq_ref, dk_ref, dv_ref, o0_ref, o1_ref, aq, ak, av, ab, xp, vec, turn = refs[skip:]
+def back_body(rows, planes, group, skip, at_ref, x_ref, qt_ref, q_ref, k_ref, v_ref, mt_ref, dt_ref, d_ref, lt_ref, *refs):
+    dq_ref, dk_ref, dv_ref, o0_ref, o1_ref, aq, ak, av, ab, row, xp, vec, turn = refs[skip:]
     w, pad = k_ref.shape[2], k_ref.shape[1]
     width = x_ref.shape[-1]
     hs = width // HEADS
@@ -509,10 +511,8 @@
 
     @pl.when(step == 0)
     def _():
-        aq[...] = jnp.zeros_like(aq)
-        ak[...] = jnp.zeros_like(ak)
-        av[...] = jnp.zeros_like(av)
-        ab[...] = jnp.zeros_like(ab)
+        for a in (aq, ak, av, ab, row):
+            a[...] = jnp.zeros_like(a)
         xp[top:, :] = jnp.zeros((pad - top, width), bf16)
 
     xp[:rows, :] = x_ref[0]
@@ -529,36 +529,49 @@
         gsc = (p * (nn(vs, ds) - delta)).astype(bf16)
         return p.astype(bf16), gsc
 
-    same = (lax.broadcasted_iota(jnp.int32, (w, 128), 0) // hs
-            == lax.broadcasted_iota(jnp.int32, (w, 128), 1) // left)
-    tile = lambda a: jnp.where(same, jnp.concatenate([a] * heads, 1), 0).astype(bf16)
+    def own_block(shape, rows_per, lanes_per):
+        return (lax.broadcasted_iota(jnp.int32, shape, 0) // rows_per
+                == lax.broadcasted_iota(jnp.int32, shape, 1) // lanes_per)
+
+    flat = own_block((w, 128), hs, left)
+    tall = own_block((128, w), left, hs)
+    tile = lambda a: jnp.where(flat, jnp.concatenate([a] * heads, 1), 0).astype(bf16)
+    pile = lambda a: jnp.where(tall, jnp.concatenate([a] * heads, 0), 0).astype(bf16)
     ql, dl, ml = (tile(ref[0, :, main:pad]) for ref in (qt_ref, dt_ref, mt_ref))
     ll = jnp.concatenate([lt_ref[0, 0, h : h + 1, main:pad] for h in range(heads)], 1)
     p, gsc = core(k, ql, v, dl, ll, ml)
-    dv_left = nt(dl, p)
-    dk_left = nt(ql, gsc) * (1.0 / LOG2E)
+    dv_left = nn(p, pile(d_ref[0, main:pad, :]))
+    dk_left = nn(gsc, pile(q_ref[0, main:pad, :]))
     dq_left = nn(kt, gsc)
-    for h in range(heads):
-        c = slice(hs * h, hs * h + hs)
-        q, d = qt_ref[0, c, :main], dt_ref[0, c, :main]
-        p, gsc = core(k[:, c], q, v[:, c], d, lt_ref[0, 0, h : h + 1, :main], mt_ref[0, c, :main])
-        dv_ref[0, c, :pad] = (nt(d, p) + dv_left[c]).astype(bf16)
-        dk_ref[0, c, :pad] = (nt(q, gsc) * (1.0 / LOG2E) + dk_left[c]).astype(bf16)
-        dq_ref[0, c, :main] = (nn(kt[c], gsc) * scale).astype(bf16)
-        dq_ref[0, c, main:pad] = (dq_left[c, left * h : left * h + left] * scale).astype(bf16)
+    even = lax.broadcasted_iota(jnp.int32, (pad, 2 * hs), 1) < hs
+    for pair in range(heads // 2):
+        both = slice(2 * hs * pair, 2 * hs * pair + 2 * hs)
+        q, d = q_ref[0, :main, both], d_ref[0, :main, both]
+        dk, dv = [], []
+        for h in (2 * pair, 2 * pair + 1):
+            c = slice(hs * h, hs * h + hs)
+            p, gsc = core(k[:, c], qt_ref[0, c, :main], v[:, c], dt_ref[0, c, :main], lt_ref[0, 0, h : h + 1, :main], mt_ref[0, c, :main])
+            dv.append(nn(p, d))
+            dk.append(nn(gsc, q))
+            dq_ref[0, c, :main] = (nn(kt[c], gsc) * scale).astype(bf16)
+            dq_ref[0, c, main:pad] = (dq_left[c, left * h : left * h + left] * scale).astype(bf16)
+        dv = jnp.where(even, *dv) + dv_left[:, both]
+        row[:, both] += fold(dv)
+        dv_ref[0, :, both] = dv.astype(bf16)
+        dk_ref[0, :, both] = ((jnp.where(even, *dk) + dk_left[:, both]) * (1.0 / LOG2E)).astype(bf16)
     x = xp[...]
     aq[...] += nn(dq_ref[0, :, :pad], x)
-    ak[...] += nn(dk_ref[0, :, :pad], x)
-    av[...] += nn(dv_ref[0, :, :pad], x)
+    ak[...] += tn(dk_ref[0], x)
+    av[...] += tn(dv_ref[0], x)
     ab[:, 0:1] += jnp.sum(dq_ref[0, :, :pad].astype(f32), 1, keepdims=True)
-    ab[:, 1:2] += jnp.sum(dv_ref[0, :, :pad].astype(f32), 1, keepdims=True)
 
     @pl.when(step == pl.num_programs(0) - 1)
     def _():
         size = width // (planes * INNER)
         n = width // planes
         vec[...] = jnp.zeros_like(vec)
-        vec[:, group * w : group * w + w] = ab[...].T
+        vec[0:1, group * w : group * w + w] = ab[...].T[0:1]
+        vec[1:2, group * w : group * w + w] = jnp.sum(row[...], 0, keepdims=True)
         for i, a in enumerate((aq, ak, av)):
             turn[i] = a[...].T
         for half, o_ref in enumerate((o0_ref, o1_ref)):
@@ -568,13 +581,14 @@
                     plane = lax.rem(at_ref[1] + planes - s, planes)
                     start = pl.multiple_of(plane * n + (at_ref[0] ^ peer) * size, size)
                     for i in range(3):
-                        o_ref[hi, s, size * i : size * i + size, :] = turn[i, pl.ds(start, size), :].astype(bf16)
-                    o_ref[hi, s, 3 * size :, :] = jnp.zeros((16, w), bf16)
+                        r, c = size * (i // 2), w * (i % 2)
+                        o_ref[hi, s, r : r + size, c : c + w] = turn[i, pl.ds(start, size), :].astype(bf16)
                     mine = vec[:, pl.ds(pl.multiple_of(plane * n, n), n)]
-                    o_ref[hi, s, 3 * size :, :n] = vector_rows(mine, at_ref[0] ^ peer, 16).astype(bf16)
-
-
-def back(at, sequence, qt, k, v, mt, dt, lt, group, planes, after=()):
+                    mine = jnp.concatenate([vector_rows(mine, at_ref[0] ^ peer, size), jnp.zeros((size, w - n), f32)], 1)
+                    o_ref[hi, s, size:, w:] = mine.astype(bf16)
+
+
+def back(at, sequence, qt, q, k, v, mt, dt, d, lt, group, planes, after=()):
     spans, rows, width = sequence.shape
     pad = k.shape[1]
     wide = qt.shape[2]
@@ -582,25 +596,26 @@
     tr = pl.BlockSpec((1, w, wide), lambda i, *_: (i, group, 0))
     nat = pl.BlockSpec((1, pad, w), lambda i, *_: (i, 0, group))
     grad = pl.BlockSpec((1, w, wide), lambda i, *_: (i, 0, 0))
-    half = (INNER // 2, planes, 3 * width // (planes * INNER) + 16, w)
+    nat_grad = pl.BlockSpec((1, pad, w), lambda i, *_: (i, 0, 0))
+    half = (INNER // 2, planes, 2 * width // (planes * INNER), 2 * w)
     out = pl.BlockSpec(half, lambda i, *_: (0, 0, 0, 0))
     return pl.pallas_call(
         functools.partial(back_body, rows, planes, group, len(after)),
         grid_spec=pltpu.PrefetchScalarGridSpec(
             num_scalar_prefetch=1,
             grid=(spans,),
-            in_specs=[pl.BlockSpec((1, rows, width), lambda i, *_: (i, 0, 0)), tr,
-                      nat, nat, tr, tr,
+            in_specs=[pl.BlockSpec((1, rows, width), lambda i, *_: (i, 0, 0)), tr, nat, nat, nat, tr, tr, nat,
                       pl.BlockSpec((1, 1, HEADS // GROUPS, wide), lambda i, *_: (i, group, 0, 0))] + [ANY] * len(after),
-            out_specs=[grad] * 3 + [out] * 2,
+            out_specs=[grad, nat_grad, nat_grad] + [out] * 2,
             scratch_shapes=[pltpu.VMEM((w, width), f32)] * 3
-            + [pltpu.VMEM((w, 8), f32), pltpu.VMEM((pad, width), bf16), pltpu.VMEM((8, width), f32), pltpu.VMEM((3, width, w), f32)],
+            + [pltpu.VMEM((w, 8), f32), pltpu.VMEM((8, w), f32), pltpu.VMEM((pad, width), bf16), pltpu.VMEM((8, width), f32),
+               pltpu.VMEM((3, width, w), f32)],
         ),
-        out_shape=[shape((spans, w, wide), bf16)] * 3 + [shape(half, bf16)] * 2,
+        out_shape=[shape((spans, w, wide), bf16)] + [shape((spans, pad, w), bf16)] * 2 + [shape(half, bf16)] * 2,
         compiler_params=params(),
         cost_estimate=cost(21),
         name=f"back{group}",
-    )(at, sequence, qt, k, v, mt, dt, lt, *after)
+    )(at, sequence, qt, q, k, v, mt, dt, d, lt, *after)
 
 
 def input_body(rows, groups, skip, *refs):
@@ -613,15 +628,15 @@
 
     @pl.when(pl.program_id(0) == 0)
     def _():
-        for a, b in zip(wt, ws):
-            a[...] = b[...].T
+        wt[0][...] = ws[0][...].T
 
     total = gs_ref[0]
     for g in range(groups):
-        for n in range(3):
-            part = parts[3 * g + n]
-            w = part.shape[1]
-            total = total + tn(part[0, :, : total.shape[0]], wt[n][w * g : w * g + w, :])
+        dq, dk, dv = (ref[0] for ref in parts[3 * g : 3 * g + 3])
+        cols = slice(dq.shape[0] * g, dq.shape[0] * g + dq.shape[0])
+        total = total + tn(dq[:, : total.shape[0]], wt[0][cols, :])
+        total = total + nt(dk, ws[1][:, cols])
+        total = total + nt(dv, ws[2][:, cols])
     out_ref[0] = total[:rows]
 
 
@@ -635,74 +650,66 @@
         in_specs=[ANY] * len(after) + [spec(gs)] + [spec(a) for a in flat] + [whole(w) for w in (wq, wk, wv)],
         out_specs=pl.BlockSpec((1, rows, width), lambda i: (i, 0, 0)),
         out_shape=shape((spans, rows, width), f32),
-        scratch_shapes=[pltpu.VMEM((width, width), bf16)] * 3,
+        scratch_shapes=[pltpu.VMEM((width, width), bf16)],
         compiler_params=params(),
         cost_estimate=cost(10),
         name="input_grad",
     )(*after, gs, *flat, wq, wk, wv)
 
 
-def ffn_final_body(cut_in, cut_back, skip, at_ref, *refs):
+def final_body(cut_in, cut_back, at_ref, *refs):
     pieces = refs[:INNER]
-    wi_ref, wb_ref, wo_ref, bin_ref, *vec_refs = refs[INNER + skip :]
+    wi_ref, wb_ref, wo_ref, wq_ref, wk_ref, wv_ref, bin_ref, *vec_refs = refs[INNER:]
     n, width = wo_ref.shape
     size = n // INNER
+    w = width // GROUPS
     for q in range(INNER):
         slot = at_ref[0] ^ (q // (INNER // 2) + 2 * (q % (INNER // 2)))
+        small = pl.ds(pl.multiple_of(slot * size, size), size)
         p = pieces[q]
         wi_ref[pl.ds(pl.multiple_of(slot * cut_in, cut_in), cut_in), :] = p[:cut_in, :].astype(f32)
         at = cut_in
         wb_ref[pl.ds(pl.multiple_of(slot * cut_back, cut_back), cut_back), :] = p[at : at + cut_back, :].astype(f32)
         at += cut_back
-        wo_ref[pl.ds(pl.multiple_of(slot * size, size), size), :] = p[at : at + size, :].astype(f32)
-        tail = p[at + size :, :].astype(f32)[0:1]
+        wo_ref[small, :] = p[at : at + size, :].astype(f32)
+        at += size
+        tail = p[at : at + 16, :].astype(f32)[0:1]
+        at += 16
+        pair = jnp.zeros((1, n), f32)
+        for g in range(GROUPS):
+            for i, o_ref in enumerate((wq_ref, wk_ref, wv_ref)):
+                r, c = at + size * (i // 2), w * (i % 2)
+                o_ref[small, w * g : w * g + w] = p[r : r + size, c : c + w].astype(f32)
+            pair = pair + p[at + size : at + 2 * size, w : w + n].astype(f32)[0:1]
+            at += 2 * size
         for i, v_ref in enumerate(vec_refs):
 
-            @pl.when(slot == i)
+            @pl.when(slot == i % 6)
             def _():
-                v_ref[...] = tail[:, :n]
-
-        @pl.when(slot == len(vec_refs))
+                v_ref[...] = tail[:, :n] if i < 6 else pair
+
+        @pl.when(slot == 6)
         def _():
             bin_ref[...] = tail
 
 
-def attend_final_body(skip, at_ref, *refs):
-    pieces = refs[:INNER]
-    wq_ref, wk_ref, wv_ref, *vec_refs = refs[INNER + skip :]
-    n, width = wq_ref.shape
-    size = n // INNER
-    w = width // GROUPS
-    for q in range(INNER):
-        slot = at_ref[0] ^ (q // (INNER // 2) + 2 * (q % (INNER // 2)))
-        p = pieces[q]
-        for i, o_ref in enumerate((wq_ref, wk_ref, wv_ref)):
-            o_ref[pl.ds(pl.multiple_of(slot * size, size), size), :] = p[size * i : size * i + size, :].astype(f32)
-        tail = p[3 * size :, :].astype(f32)[0:1]
-        pair = tail[:, :n]
-        for g in range(1, GROUPS):
-            pair = pair + tail[:, w * g : w * g + n]
-        for i, v_ref in enumerate(vec_refs):
-
-            @pl.when(slot == i)
-            def _():
-                v_ref[...] = pair
-
-
-def final(body, at, pieces, out, after, name):
-    return pl.pallas_call(
-        functools.partial(body, len(after)),
+def final(at, pieces, own, planes):
+    width = pieces[0].shape[1]
+    n = width // planes
+    out = [(width, own), (own, width)] + [(n, width)] * 4 + [(1, own)] + [(1, n)] * 8
+    return pl.pallas_call(
+        functools.partial(final_body, width // INNER, own // INNER),
         grid_spec=pltpu.PrefetchScalarGridSpec(
             num_scalar_prefetch=1,
             grid=(1,),
-            in_specs=[whole(a) for a in pieces] + [ANY] * len(after),
+            in_specs=[whole(a) for a in pieces],
             out_specs=[pl.BlockSpec(d, lambda *_: (0, 0)) for d in out],
         ),
         out_shape=[shape(d, f32) for d in out],
         compiler_params=params(),
         cost_estimate=cost(3),
-        name=name,
-    )(at, *pieces, *after)
+        name="final",
+    )(at, *pieces)
 
 
 def shards(dp, planes, sequence, cotangent, w_query, b_query, w_key, w_value, b_value, w_out, b_out, gain_attn, shift_attn,
@@ -722,9 +729,11 @@
         far = lax.optimization_barrier((*far, *after))[: INNER // 2]
         return list(far) + [swap(b, 1) for b in far]
 
-    def in_plane(parts, after, name):
-        parts = [parts[0]] + [swap(parts[k], 2 * k) for k in range(1, INNER // 2)]
-        totals = plane_sum(parts, after, name)
+    def from_plane(parts):
+        return [parts[0]] + [swap(parts[k], 2 * k) for k in range(1, INNER // 2)]
+
+    def outer(totals):
+        totals = list(totals)
         step = INNER
         while step < dp:
             totals = [(t.astype(f32) + swap(t, step).astype(f32)).astype(bf16) for t in totals]
@@ -741,28 +750,22 @@
     head = 1
     first = attend(*common, 0, head)
     far, bias_far = join(far, first[:1])
-    qt, k, v, mt, lt, so = attend(*common, head, spans - head, first, (far,))
+    qt, k, v, mt, lt, so, q = attend(*common, head, spans - head, first, (far,))
     far = spread(far, (so,))
-    layer_out, gs, ga, dt, keep, send = ffn(at, so, cotangent, mt, vec, w_out, b_in, bias_far, w_in, w_back, far)
-    *grad0, keep0, send0 = back(at, sequence, qt, k, v, mt, dt, lt, 0, planes)
-    ffn_parts = core_sum([(keep, swap(send, 1))], 1, (keep0,), "core_ffn")
-    *grad1, keep1, send1 = back(at, sequence, qt, k, v, mt, dt, lt, 1, planes, (ffn_parts[0],))
-    ffn_parts = to_planes(in_plane(ffn_parts, (keep1,), "plane_ffn"))
-    parts = core_sum([(keep0, swap(send0, 1)), (keep1, swap(send1, 1))], 2, (ffn_parts[0],), "core_attn")
-    by_input = input_grad(rows, gs, [grad0, grad1], w_query, w_key, w_value, (ffn_parts[0],))
-    layer_out = lax.optimization_barrier(jnp.transpose(layer_out, (1, 0, 2)))
-    totals = in_plane(parts, (by_input, layer_out), "plane_attn")
-    ffn_sum = last_sum([ffn_parts], (totals[0],), "last_ffn")
-    by_input = lax.optimization_barrier((by_input, ffn_sum))[0]
-    by_input = lax.optimization_barrier(jnp.transpose(by_input, (1, 0, 2)))
-    ffn_pieces = spread(ffn_sum)
-    attn_sum = last_sum([to_planes(totals)], (ffn_sum, by_input), "last_attn")
-    n = width // planes
-    wi, wb, wo, bins, gg2, gs2, bb, gg1, gs1, bo = final(
-        functools.partial(ffn_final_body, width // INNER, own // INNER), at, ffn_pieces,
-        [(width, own), (own, width), (n, width), (1, own)] + [(1, n)] * 6, (attn_sum,), "ffn_final")
-    attn_pieces = spread(attn_sum, (wi,))
-    wq, wk, wv, bq, bv = final(attend_final_body, at, attn_pieces, [(n, width)] * 3 + [(1, n)] * 2, (), "attend_final")
+    layer_out, gs, d, dt, keep, send = ffn(at, so, cotangent, mt, vec, w_out, b_in, bias_far, w_in, w_back, far)
+    *grad0, keep0, send0 = back(at, sequence, qt, q, k, v, mt, dt, d, lt, 0, planes)
+    got0 = swap(send0, 1)
+    ffn_parts = core_sum([(keep, swap(send, 1))], (keep0,), "core_ffn")
+    *grad1, keep1, send1 = back(at, sequence, qt, q, k, v, mt, dt, d, lt, 1, planes, (ffn_parts[0], got0))
+    ffn_parts = from_plane(ffn_parts)
+    parts = core_sum([(keep0, got0), (keep1, swap(send1, 1))], ffn_parts[1:], "core_attn")
+    ffn_totals = to_planes(outer(plane_sum(ffn_parts, (parts[0],), "plane_ffn")))
+    by_input = input_grad(rows, gs, [grad0, grad1], w_query, w_key, w_value, (ffn_totals[0],))
+    totals = to_planes(outer(plane_sum(from_plane(parts), (by_input,), "plane_attn")))
+    layer_out, by_input = lax.optimization_barrier((layer_out, by_input, totals[0]))[:2]
+    layer_out, by_input = (lax.optimization_barrier(jnp.transpose(a, (1, 0, 2))) for a in (layer_out, by_input))
+    pieces = spread(last_sum([ffn_totals, totals], (by_input, layer_out), "last"))
+    wi, wb, wo, wq, wk, wv, bins, gg2, gs2, bb, gg1, gs1, bo, bq, bv = final(at, pieces, own, planes)
     row = lambda a: a.reshape(-1)
     layer_out, by_input = (jnp.transpose(a, (1, 0, 2)) for a in (layer_out, by_input))
     return (layer_out, by_input, wq, row(bq), wk, wv, row(bv), wo, row(bo), row(gg1), row(gs1), wi, row(bins), wb,

time: 243 us -> 235 us (0.967)
  Pallas kernels: 168 us -> 160 us
  waiting for transfers between devices: 11.7 us -> 17.2 us
  starting transfers between devices: 34.1 us -> 30.7 us
    ppermute x30 -> x23, waiting for transfers between devices: 8.09 us -> 16.3 us  [swap(): return lax.ppermute(a, 'dp', [(i, i ^ k) for i in range(dp)])]
    ppermute x30 -> x23, starting transfers between devices: 21.5 us -> 16.9 us  [swap(): return lax.ppermute(a, 'dp', [(i, i ^ k) for i in range(dp)])]
    pallas_call x1, Pallas kernels: 63.3 us -> 59 us  [ffn(): pl.pallas_call(functools.partial(ffn_body, rows, len(far), planes), grid_...]
    ppermute x9, waiting for transfers between devices: 3.59 us -> 0.91 us  [turn(): return lax.ppermute(a, 'mp', [(i, (i + s) % planes) for i in range(planes)])]
    pallas_call x1 -> x0, local copies, waits for them, and re-layouts: 2.47 us -> none  [ffn(): pl.pallas_call(functools.partial(ffn_body, rows, len(far), planes), grid_...]
    optimization_barrier x1 -> x2, local copies, waits for them, and re-layouts: 7.16 us -> 9.58 us  [shards(): lax.optimization_barrier((layer_out, by_input, totals[0]))[:2]]
    pallas_call x4 -> x3, Pallas kernels: 14.9 us -> 12.5 us  [the longest x2 8.11 us: core_sum(): pl.pallas_call(functools.partial(core_sum_body, len(pairs), len(after)),...]
    unnamed x96 -> x78, local copies, waits for them, and re-layouts: 13 us -> 12.3 us
  transfers between devices with their start and end apart: 39 -> 32, of which waited for: 9 -> 11; matrix products, arithmetic and copies ran while one was open for 6% -> 6% of each run, Pallas kernels for 40% -> 37%
where the time goes in v1:
time: 235 us; the launch traced here: 231 us
  Pallas kernels  160 us (68%)
  starting transfers between devices  30.7 us (13%)
  local copies, waits for them, and re-layouts  21.8 us (9%)
  waiting for transfers between devices  17.2 us (7%)
    pallas_call x1, Pallas kernels, ffn(): pl.pallas_call(functools.partial(ffn_body, rows, len(far), planes), grid_...  59 us
    pallas_call x2, Pallas kernels, back(): pl.pallas_call(functools.partial(back_body, rows, planes, group, len(afte...  41.6 us
    pallas_call x2, Pallas kernels, attend(): pl.pallas_call(functools.partial(attend_body, rows, pad, len(before) + le...  24.8 us
    ppermute x23, starting transfers between devices, swap(): return lax.ppermute(a, 'dp', [(i, i ^ k) for i in range(dp)])  16.9 us
    ppermute x23, waiting for transfers between devices, swap(): return lax.ppermute(a, 'dp', [(i, i ^ k) for i in range(dp)])  16.3 us
    ppermute x9, starting transfers between devices, turn(): return lax.ppermute(a, 'mp', [(i, (i + s) % planes) for i in range(planes)])  13.7 us
    unnamed x78, local copies, waits for them, and re-layouts  12.3 us
    optimization_barrier x2, local copies, waits for them, and re-layouts, shards(): lax.optimization_barrier((layer_out, by_input, totals[0]))[:2]  9.58 us
  transfers between devices with their start and end apart: 32, of which 11 were waited for; matrix products, arithmetic and copies ran while one was open for 6% of the time, Pallas kernels for 37%

profile of v1, /device:TPU:0, one launch (start us, length us, event | category | flops | bytes accessed | tf_op | source)
XLA Modules:
  0.0 231.1 jit_solution(17720889467384367768)
XLA Ops:
  1.2 2.3 %prep.1.refs_8_ = bf16[144,512]{1,0:T(8,128)(2,1)} custom-call(s32[2]{0:T(128)} %pad_add_fusion.at_ref, bf16[512,512]{1,0:T(8,128)(2,1)} %wi_ref.3, bf16[512,512]{1,0:T(8,128)(2,1)} %wb_ref.3, bf16[512]{0:T(512)(128)(2,1)} %bi_ref.3), custom_call_target="tpu_custom_call" | custom-call | flops 2000000000 | bytes 200000 | tf_op jit(solution)/shard_map/prep/pallas_call | solution.py:79
  3.6 5.0 %collective-permute-start.2 = (bf16[144,512]{1,0:T(8,128)(2,1)}, bf16[144,512]{1,0:T(8,128)(2,1)S(1)}, u32[]{:S(2)}, u32[]{:S(2)}) collective-permute-start(bf16[144,512]{1,0:T(8,128)(2,1)} %prep.1.refs_8_), channel_id=1, source_target_pairs={{0,3},{1,0},{2,1},{3,2},{4,7},{5,4},{6,5},{7,6},{8,11},{9,8},{10,9... | collective-permute-start | bytes 442376 | tf_op jit(solution)/shard_map/ppermute | solution.py:725
  9.6 1.8 copy.42.x_ref
  12.8 7.6 %attend0.1 = (bf16[4,512,640]{2,1,0:T(8,128)(2,1)}, bf16[4,544,512]{2,1,0:T(8,128)(2,1)}, bf16[4,544,512]{2,1,0:T(8,128)(2,1)}, bf16[4,512,640]{2,1,0:T(8,128)(2...) custom-call(bf16[4,532,512]{2,1,0:T(8,128)(2,1)} %copy.42.x_ref, ...), custom_call_target="tpu_custom_call" | custom-call | flops 16000000000 | bytes 1600000 | tf_op jit(solution)/shard_map/attend0/pallas_call | solution.py:179
  22.0 1.8 join.1
  23.8 2.4 %collective-permute-start.5 = (bf16[3,128,512]{2,1,0:T(8,128)(2,1)}, bf16[3,128,512]{2,1,0:T(8,128)(2,1)S(1)}, u32[]{:S(2)}, u32[]{:S(2)}) collective-permute-start(bf16[3,128,512]{2,1,0:T(8,128)(2,1)} %get-tuple-element.101.refs_7_.refs_0_), channel_id=1, source_target_pairs={{0,24},{4,28},{8,16},{12,20},{16,8},{20,12},{24,0},{28,4},{1,25},{... | collective-permute-start | bytes 1179656 | tf_op jit(solution)/shard_map/ppermute | solution.py:722
  27.3 17.2 %attend1.1 = (bf16[4,512,640]{2,1,0:T(8,128)(2,1)}, bf16[4,544,512]{2,1,0:T(8,128)(2,1)}, bf16[4,544,512]{2,1,0:T(8,128)(2,1)}, bf16[4,512,640]{2,1,0:T(8,128)(2...) custom-call(bf16[4,532,512]{2,1,0:T(8,128)(2,1)} %copy.42.x_ref, ...), custom_call_target="tpu_custom_call", output_to_operand_aliasing={{0}: (6, {}), {1}: (7, {}), {2}: (8, {}), {3}: (9, {}), {4}... | custom-call | flops 16000000000 | bytes 1600000 | tf_op jit(solution)/shard_map/attend1/pallas_call | solution.py:179
  49.0 59.0 %ffn.1 = (bf16[4,532,512]{2,1,0:T(8,128)(2,1)}, f32[4,544,512]{2,1,0:T(8,128)}, bf16[4,544,512]{2,1,0:T(8,128)(2,1)}, bf16[4,512,640]{2,1,0:T(8,128)(2,1)}, bf16...) custom-call(s32[2]{0:T(128)} %pad_add_fusion.at_ref, f32[4,544,512]{2,1,0:T(8,128)} %get-tuple-element.98.so_ref, ...), custom_call_target="tpu_custom_call" | custom-call | flops 46000001024 | bytes 4600000 | tf_op jit(solution)/shard_map/ffn/pallas_call | solution.py:386
  108.1 20.8 %back0.1 = (bf16[4,256,640]{2,1,0:T(8,128)(2,1)}, bf16[4,544,256]{2,1,0:T(8,128)(2,1)}, bf16[4,544,256]{2,1,0:T(8,128)(2,1)}, bf16[4,4,32,512]{3,2,1,0:T(8,128)(2,1)}, bf16[4,4,32,512]{3,2,1,0:T(8,128)(2,1)}) custom-call(s32[2]{0:T(128)} %pad_add_fusion.at_ref, bf16[4,532,512]{2,1,0:T(8,128)(2,1)} %copy.42.x_ref, ...), custom_call_target="tpu_custom_call" | custom-call | flops 20999999488 | bytes 2100000 | tf_op jit(solution)/shard_map/back0/pallas_call | solution.py:602
  130.9 4.5 %core_ffn.1 = (bf16[4,160,512]{2,1,0:T(8,128)(2,1)}, bf16[4,160,512]{2,1,0:T(8,128)(2,1)}, bf16[4,160,512]{2,1,0:T(8,128)(2,1)}, bf16[4,160,512]{2,1,0:T(8,128)(2,1)}) custom-call(bf16[4,4,160,512]{3,2,1,0:T(8,128)(2,1)} %get-tuple-element.106.refs_0_, bf16[4,4,160,512]{3,2,1,0:T(8,128)(2,1)} %copy-done, ...), custom_call_target="tpu_custom_call" | custom-call | flops 1000000 | bytes 100 | tf_op jit(solution)/shard_map/core_ffn/pallas_call | solution.py:446
  139.7 20.8 %back1.1 = (bf16[4,256,640]{2,1,0:T(8,128)(2,1)}, bf16[4,544,256]{2,1,0:T(8,128)(2,1)}, bf16[4,544,256]{2,1,0:T(8,128)(2,1)}, bf16[4,4,32,512]{3,2,1,0:T(8,128)(2,1)}, bf16[4,4,32,512]{3,2,1,0:T(8,128)(2,1)}) custom-call(s32[2]{0:T(128)} %pad_add_fusion.at_ref, bf16[4,532,512]{2,1,0:T(8,128)(2,1)} %copy.42.x_ref, ...), custom_call_target="tpu_custom_call" | custom-call | flops 20999999488 | bytes 2100000 | tf_op jit(solution)/shard_map/back1/pallas_call | solution.py:602
  160.6 2.1 collective-permute-done.15.refs_3_
  162.7 4.9 %collective-permute-done.12.refs_5_.refs_2_ = bf16[4,160,512]{2,1,0:T(8,128)(2,1)S(1)} collective-permute-done((bf16[4,160,512]{2,1,0:T(8,128)(2,1)}, bf16[4,160,512]{2,1,0:T(8,128)(2,1)S(1)}, u32[]{:S(2)}, u32[]{:S(2)}) %collective-permute-start.12) | collective-permute-done | bytes 655392 | tf_op jit(solution)/shard_map/ppermute | solution.py:722
  168.6 3.6 %core_attn.1 = (bf16[4,64,512]{2,1,0:T(8,128)(2,1)}, bf16[4,64,512]{2,1,0:T(8,128)(2,1)}, bf16[4,64,512]{2,1,0:T(8,128)(2,1)}, bf16[4,64,512]{2,1,0:T(8,128)(2,1)}) custom-call(bf16[4,4,32,512]{3,2,1,0:T(8,128)(2,1)} %get-tuple-element.115.refs_2_.refs_0_, bf16[4,4,32,512]{3,2,1,0:T(8,128)(2,1)} %copy-done.7, ...), custom_call_target="tpu_custom_call" | custom-call | flops 1000000 | bytes 100 | tf_op jit(solution)/shard_map/core_attn/pallas_call | solution.py:446
  173.3 2.7 %plane_ffn.1 = (bf16[160,512]{1,0:T(8,128)(2,1)}, bf16[160,512]{1,0:T(8,128)(2,1)}, bf16[160,512]{1,0:T(8,128)(2,1)}, bf16[160,512]{1,0:T(8,128)(2,1)}) custom-call(bf16[4,160,512]{2,1,0:T(8,128)(2,1)} %get-tuple-element.116.refs_0_, bf16[4,160,512]{2,1,0:T(8,128)(2,1)} %copy-done.1, bf16[4,160,512]{2,1,0:T(8,128)(2,1)} %copy-done.2, ...), custom_call_target="tpu_custom_call" | custom-call | flops 1000000 | bytes 100 | tf_op jit(solution)/shard_map/plane_ffn/pallas_call | solution.py:466
  176.0 2.0 collective-permute-start.19
  183.3 9.6 %input_grad.1.refs_4_ = f32[4,532,512]{2,1,0:T(8,128)} custom-call(bf16[160,512]{1,0:T(8,128)(2,1)} %get-tuple-element.124.refs_0_, f32[4,544,512]{2,1,0:T(8,128)} %get-tuple-element.125.refs_1_, bf16[4,256,640]{2,1,0:T(8,128)(2,1)} %get-tuple-element.126.refs_2_, bf16[4,544,256]{2,1,0:T(8,128)(2,1)} %get-tuple-element.127.refs_3_, ...), custom_call_target="tpu_custom_call" | custom-call | flops 10000000000 | bytes 1000000 | tf_op jit(solution)/shard_map/input_grad/pallas_call | solution.py:647
  194.3 1.9 plane_attn.1
  196.3 2.1 collective-permute-start.22
  199.2 2.5 %copy.51 = bf16[4,532,512]{2,0,1:T(4,128)(2,1)} copy(bf16[4,532,512]{2,1,0:T(8,128)(2,1)S(1)} %copy-done.4) | data formatting | bytes 4358144 | tf_op jit(solution)/shard_map/optimization_barrier | solution.py:765
  201.6 7.1 %copy.50 = f32[4,532,512]{2,0,1:T(4,128)} copy(f32[4,532,512]{2,1,0:T(8,128)} %input_grad.1.refs_4_) | data formatting | bytes 8716288 | tf_op jit(solution)/shard_map/optimization_barrier | solution.py:765
  210.1 2.0 last.1.refs_0_
  215.6 5.7 %collective-permute-done.27.refs_3_ = bf16[224,512]{1,0:T(8,128)(2,1)S(1)} collective-permute-done((bf16[224,512]{1,0:T(8,128)(2,1)}, bf16[224,512]{1,0:T(8,128)(2,1)S(1)}, u32[]{:S(2)}, u32[]{:S(2)}) %collective-permute-start.27) | collective-permute-done | bytes 229408 | tf_op jit(solution)/shard_map/ppermute | solution.py:722
  226.5 4.4 %final.1 = (f32[512,512]{1,0:T(8,128)}, f32[512,512]{1,0:T(8,128)}, f32[128,512]{1,0:T(8,128)}, f32[128,512]{1,0:T(8,128)}, f32[128,512]{1,0:T(8,128)}, /*index=...) custom-call(s32[2]{0:T(128)} %pad_add_fusion.at_ref, ...), custom_call_target="tpu_custom_call" | custom-call | flops 3000000000 | bytes 300000 | tf_op jit(solution)/shard_map/final/pallas_call | solution.py:700
  (136 shorter events, 36.0 us)
Async XLA Ops:
  3.6 16.8 %collective-permute-start.2 = (bf16[144,512]{1,0:T(8,128)(2,1)}, bf16[144,512]{1,0:T(8,128)(2,1)S(1)}, u32[]{:S(2)}, u32[]{:S(2)}) collective-permute-start(bf16[144,512]{1,0:T(8,128)(2,1)} %prep.1.refs_8_), channel_id=1, source_target_pairs={{0,3},{1,0},{2,1},{3,2},{4,7},{5,4},{6,5},{7,6},{8,11},{9,8},{10,9... | collective-permute-start | bytes 442376 | tf_op jit(solution)/shard_map/ppermute | solution.py:725
  8.6 12.7 %collective-permute-start.1 = (bf16[144,512]{1,0:T(8,128)(2,1)}, bf16[144,512]{1,0:T(8,128)(2,1)S(1)}, u32[]{:S(2)}, u32[]{:S(2)}) collective-permute-start(bf16[144,512]{1,0:T(8,128)(2,1)} %prep.1.refs_8_), channel_id=1, source_target_pairs={{0,2},{1,3},{2,0},{3,1},{4,6},{5,7},{6,4},{7,5},{8,10},{9,11},{10,... | collective-permute-start | bytes 442376 | tf_op jit(solution)/shard_map/ppermute | solution.py:725
  8.6 12.7 %collective-permute-start = (bf16[144,512]{1,0:T(8,128)(2,1)}, bf16[144,512]{1,0:T(8,128)(2,1)S(1)}, u32[]{:S(2)}, u32[]{:S(2)}) collective-permute-start(bf16[144,512]{1,0:T(8,128)(2,1)} %prep.1.refs_8_), channel_id=1, source_target_pairs={{0,1},{1,2},{2,3},{3,0},{4,5},{5,6},{6,7},{7,4},{8,9},{9,10},{10,1... | collective-permute-start | bytes 442376 | tf_op jit(solution)/shard_map/ppermute | solution.py:725
  23.8 20.7 %collective-permute-start.5 = (bf16[3,128,512]{2,1,0:T(8,128)(2,1)}, bf16[3,128,512]{2,1,0:T(8,128)(2,1)S(1)}, u32[]{:S(2)}, u32[]{:S(2)}) collective-permute-start(bf16[3,128,512]{2,1,0:T(8,128)(2,1)} %get-tuple-element.101.refs_7_.refs_0_), channel_id=1, source_target_pairs={{0,24},{4,28},{8,16},{12,20},{16,8},{20,12},{24,0},{28,4},{1,25},{... | collective-permute-start | bytes 1179656 | tf_op jit(solution)/shard_map/ppermute | solution.py:722
  26.3 18.3 %collective-permute-start.4 = (bf16[3,128,512]{2,1,0:T(8,128)(2,1)}, bf16[3,128,512]{2,1,0:T(8,128)(2,1)S(1)}, u32[]{:S(2)}, u32[]{:S(2)}) collective-permute-start(bf16[3,128,512]{2,1,0:T(8,128)(2,1)} %get-tuple-element.101.refs_7_.refs_0_), channel_id=1, source_target_pairs={{0,16},{4,20},{8,24},{12,28},{16,0},{20,4},{24,8},{28,12},{1,17},{... | collective-permute-start | bytes 1179656 | tf_op jit(solution)/shard_map/ppermute | solution.py:722
  26.8 17.8 %collective-permute-start.3 = (bf16[3,128,512]{2,1,0:T(8,128)(2,1)}, bf16[3,128,512]{2,1,0:T(8,128)(2,1)S(1)}, u32[]{:S(2)}, u32[]{:S(2)}) collective-permute-start(bf16[3,128,512]{2,1,0:T(8,128)(2,1)} %get-tuple-element.101.refs_7_.refs_0_), channel_id=1, source_target_pairs={{0,8},{4,12},{8,0},{12,4},{16,24},{20,28},{24,16},{28,20},{1,9},{5... | collective-permute-start | bytes 1179656 | tf_op jit(solution)/shard_map/ppermute | solution.py:722
  44.6 2.8 %collective-permute-start.6 = (bf16[3,128,512]{2,1,0:T(8,128)(2,1)S(1)}, bf16[3,128,512]{2,1,0:T(8,128)(2,1)S(1)}, u32[]{:S(2)}, u32[]{:S(2)}) collective-permute-start(bf16[3,128,512]{2,1,0:T(8,128)(2,1)S(1)} %copy-done.18), channel_id=1, source_target_pairs={{0,4},{4,0},{8,12},{12,8},{16,20},{20,16},{24,28},{28,24},{1,5},{5... | collective-permute-start | bytes 1179656 | tf_op jit(solution)/shard_map/ppermute | solution.py:722
  108.0 21.4 %collective-permute-start.10 = (bf16[4,4,160,512]{3,2,1,0:T(8,128)(2,1)}, bf16[4,4,160,512]{3,2,1,0:T(8,128)(2,1)S(1)}, u32[]{:S(2)}, u32[]{:S(2)}) collective-permute-start(bf16[4,4,160,512]{3,2,1,0:T(8,128)(2,1)} %get-tuple-element.107), channel_id=1, source_target_pairs={{0,4},{4,0},{8,12},{12,8},{16,20},{20,16},{24,28},{28,24},{1,5},{5... | collective-permute-start | bytes 7864328 | tf_op jit(solution)/shard_map/ppermute | solution.py:722
  128.9 10.0 %collective-permute-start.14 = (bf16[4,4,32,512]{3,2,1,0:T(8,128)(2,1)}, bf16[4,4,32,512]{3,2,1,0:T(8,128)(2,1)S(1)}, u32[]{:S(2)}, u32[]{:S(2)}) collective-permute-start(bf16[4,4,32,512]{3,2,1,0:T(8,128)(2,1)} %get-tuple-element.120), channel_id=1, source_target_pairs={{0,4},{4,0},{8,12},{12,8},{16,20},{20,16},{24,28},{28,24},{1,5},{5... | collective-permute-start | bytes 1572872 | tf_op jit(solution)/shard_map/ppermute | solution.py:722
  135.4 27.3 %collective-permute-start.11 = (bf16[4,160,512]{2,1,0:T(8,128)(2,1)}, bf16[4,160,512]{2,1,0:T(8,128)(2,1)S(1)}, u32[]{:S(2)}, u32[]{:S(2)}) collective-permute-start(bf16[4,160,512]{2,1,0:T(8,128)(2,1)} %get-tuple-element.117), channel_id=1, source_target_pairs={{0,8},{4,12},{8,0},{12,4},{16,24},{20,28},{24,16},{28,20},{1,9},{5... | collective-permute-start | bytes 1966088 | tf_op jit(solution)/shard_map/ppermute | solution.py:722
  136.9 30.7 %collective-permute-start.12 = (bf16[4,160,512]{2,1,0:T(8,128)(2,1)}, bf16[4,160,512]{2,1,0:T(8,128)(2,1)S(1)}, u32[]{:S(2)}, u32[]{:S(2)}) collective-permute-start(bf16[4,160,512]{2,1,0:T(8,128)(2,1)} %get-tuple-element.118), channel_id=1, source_target_pairs={{0,16},{4,20},{8,24},{12,28},{16,0},{20,4},{24,8},{28,12},{1,17},{... | collective-permute-start | bytes 1966088 | tf_op jit(solution)/shard_map/ppermute | solution.py:722
  138.4 29.2 %collective-permute-start.13 = (bf16[4,160,512]{2,1,0:T(8,128)(2,1)}, bf16[4,160,512]{2,1,0:T(8,128)(2,1)S(1)}, u32[]{:S(2)}, u32[]{:S(2)}) collective-permute-start(bf16[4,160,512]{2,1,0:T(8,128)(2,1)} %get-tuple-element.119), channel_id=1, source_target_pairs={{0,24},{4,28},{8,16},{12,20},{16,8},{20,12},{24,0},{28,4},{1,25},{... | collective-permute-start | bytes 1966088 | tf_op jit(solution)/shard_map/ppermute | solution.py:722
  172.2 9.6 %collective-permute-start.16 = (bf16[4,64,512]{2,1,0:T(8,128)(2,1)}, bf16[4,64,512]{2,1,0:T(8,128)(2,1)S(1)}, u32[]{:S(2)}, u32[]{:S(2)}) collective-permute-start(bf16[4,64,512]{2,1,0:T(8,128)(2,1)} %get-tuple-element.132), channel_id=1, source_target_pairs={{0,8},{4,12},{8,0},{12,4},{16,24},{20,28},{24,16},{28,20},{1,9},{5... | collective-permute-start | bytes 786440 | tf_op jit(solution)/shard_map/ppermute | solution.py:722
  176.0 22.4 %collective-permute-start.19 = (bf16[160,512]{1,0:T(8,128)(2,1)}, bf16[160,512]{1,0:T(8,128)(2,1)S(1)}, u32[]{:S(2)}, u32[]{:S(2)}) collective-permute-start(bf16[160,512]{1,0:T(8,128)(2,1)} %get-tuple-element.138), channel_id=1, source_target_pairs={{0,3},{1,0},{2,1},{3,2},{4,7},{5,4},{6,5},{7,6},{8,11},{9,8},{10,9... | collective-permute-start | bytes 491528 | tf_op jit(solution)/shard_map/ppermute | solution.py:725
  177.9 30.8 %collective-permute-start.20 = (bf16[160,512]{1,0:T(8,128)(2,1)}, bf16[160,512]{1,0:T(8,128)(2,1)S(1)}, u32[]{:S(2)}, u32[]{:S(2)}) collective-permute-start(bf16[160,512]{1,0:T(8,128)(2,1)} %get-tuple-element.139), channel_id=1, source_target_pairs={{0,2},{1,3},{2,0},{3,1},{4,6},{5,7},{6,4},{7,5},{8,10},{9,11},{10,... | collective-permute-start | bytes 491528 | tf_op jit(solution)/shard_map/ppermute | solution.py:725
  179.1 29.7 %collective-permute-start.21 = (bf16[160,512]{1,0:T(8,128)(2,1)}, bf16[160,512]{1,0:T(8,128)(2,1)S(1)}, u32[]{:S(2)}, u32[]{:S(2)}) collective-permute-start(bf16[160,512]{1,0:T(8,128)(2,1)} %get-tuple-element.140), channel_id=1, source_target_pairs={{0,1},{1,2},{2,3},{3,0},{4,5},{5,6},{6,7},{7,4},{8,9},{9,10},{10,1... | collective-permute-start | bytes 491528 | tf_op jit(solution)/shard_map/ppermute | solution.py:725
  180.8 12.1 %collective-permute-start.17 = (bf16[4,64,512]{2,1,0:T(8,128)(2,1)S(1)}, bf16[4,64,512]{2,1,0:T(8,128)(2,1)S(1)}, u32[]{:S(2)}, u32[]{:S(2)}) collective-permute-start(bf16[4,64,512]{2,1,0:T(8,128)(2,1)S(1)} %copy-done.27), channel_id=1, source_target_pairs={{0,16},{4,20},{8,24},{12,28},{16,0},{20,4},{24,8},{28,12},{1,17},{... | collective-permute-start | bytes 786440 | tf_op jit(solution)/shard_map/ppermute | solution.py:722
  181.8 11.1 %collective-permute-start.18 = (bf16[4,64,512]{2,1,0:T(8,128)(2,1)S(1)}, bf16[4,64,512]{2,1,0:T(8,128)(2,1)S(1)}, u32[]{:S(2)}, u32[]{:S(2)}) collective-permute-start(bf16[4,64,512]{2,1,0:T(8,128)(2,1)S(1)} %copy-done.26), channel_id=1, source_target_pairs={{0,24},{4,28},{8,16},{12,20},{16,8},{20,12},{24,0},{28,4},{1,25},{... | collective-permute-start | bytes 786440 | tf_op jit(solution)/shard_map/ppermute | solution.py:722
  196.3 12.5 %collective-permute-start.22 = (bf16[64,512]{1,0:T(8,128)(2,1)}, bf16[64,512]{1,0:T(8,128)(2,1)S(1)}, u32[]{:S(2)}, u32[]{:S(2)}) collective-permute-start(bf16[64,512]{1,0:T(8,128)(2,1)} %get-tuple-element.141), channel_id=1, source_target_pairs={{0,3},{1,0},{2,1},{3,2},{4,7},{5,4},{6,5},{7,6},{8,11},{9,8},{10,9... | collective-permute-start | bytes 196616 | tf_op jit(solution)/shard_map/ppermute | solution.py:725
  198.4 10.4 %collective-permute-start.23 = (bf16[64,512]{1,0:T(8,128)(2,1)}, bf16[64,512]{1,0:T(8,128)(2,1)S(1)}, u32[]{:S(2)}, u32[]{:S(2)}) collective-permute-start(bf16[64,512]{1,0:T(8,128)(2,1)} %get-tuple-element.142), channel_id=1, source_target_pairs={{0,2},{1,3},{2,0},{3,1},{4,6},{5,7},{6,4},{7,5},{8,10},{9,11},{10,... | collective-permute-start | bytes 196616 | tf_op jit(solution)/shard_map/ppermute | solution.py:725
  198.4 10.4 %collective-permute-start.24 = (bf16[64,512]{1,0:T(8,128)(2,1)}, bf16[64,512]{1,0:T(8,128)(2,1)S(1)}, u32[]{:S(2)}, u32[]{:S(2)}) collective-permute-start(bf16[64,512]{1,0:T(8,128)(2,1)} %get-tuple-element.143), channel_id=1, source_target_pairs={{0,1},{1,2},{2,3},{3,0},{4,5},{5,6},{6,7},{7,4},{8,9},{9,10},{10,1... | collective-permute-start | bytes 196616 | tf_op jit(solution)/shard_map/ppermute | solution.py:725
  212.1 9.2 %collective-permute-start.27 = (bf16[224,512]{1,0:T(8,128)(2,1)}, bf16[224,512]{1,0:T(8,128)(2,1)S(1)}, u32[]{:S(2)}, u32[]{:S(2)}) collective-permute-start(bf16[224,512]{1,0:T(8,128)(2,1)} %last.1.refs_0_), channel_id=1, source_target_pairs={{0,24},{4,28},{8,16},{12,20},{16,8},{20,12},{24,0},{28,4},{1,25},{... | collective-permute-start | bytes 688136 | tf_op jit(solution)/shard_map/ppermute | solution.py:722
  213.6 9.2 %collective-permute-start.26 = (bf16[224,512]{1,0:T(8,128)(2,1)}, bf16[224,512]{1,0:T(8,128)(2,1)S(1)}, u32[]{:S(2)}, u32[]{:S(2)}) collective-permute-start(bf16[224,512]{1,0:T(8,128)(2,1)} %last.1.refs_0_), channel_id=1, source_target_pairs={{0,16},{4,20},{8,24},{12,28},{16,0},{20,4},{24,8},{28,12},{1,17},{... | collective-permute-start | bytes 688136 | tf_op jit(solution)/shard_map/ppermute | solution.py:722
  214.6 8.2 %collective-permute-start.25 = (bf16[224,512]{1,0:T(8,128)(2,1)}, bf16[224,512]{1,0:T(8,128)(2,1)S(1)}, u32[]{:S(2)}, u32[]{:S(2)}) collective-permute-start(bf16[224,512]{1,0:T(8,128)(2,1)} %last.1.refs_0_), channel_id=1, source_target_pairs={{0,8},{4,12},{8,0},{12,4},{16,24},{20,28},{24,16},{28,20},{1,9},{5... | collective-permute-start | bytes 688136 | tf_op jit(solution)/shard_map/ppermute | solution.py:722
  (46 other events, 156.8 us)

commit v2 on v1

--- a/solution.py
+++ b/solution.py
@@ -200,7 +200,7 @@
 
 
 def ffn_body(rows, slices, planes, at_ref, so_ref, ct_ref, mt_ref, vec_ref, wo_ref, bi_ref, bf_ref, wi_ref, wb_ref, *refs):
-    (lo_ref, gs_ref, d_ref, dot_ref, o0_ref, o1_ref,
+    (lo_ref, gs_ref, d_ref, dot_ref, o0_ref, o1_ref, side_ref,
      col, binv, wi, wb, one, two, inv1, act, pre_grad, low, grad, acc, turn, low_grad, sem) = refs[slices:]
     pad, width = so_ref.shape[1:]
     own = wb_ref.shape[0]
@@ -368,7 +368,9 @@
                 slot = slot_of(half, hi)
                 start = pl.multiple_of(plane * n + slot * size, size)
                 outs[half][hi, s, at : at + size, :] = acc[pl.ds(start, size), :].astype(bf16)
-                outs[half][hi, s, at + size :, :] = vector_rows(mine, slot, 16).astype(bf16)
+                row = vector_rows(mine, slot, 8)
+                w = width // 2
+                side_ref[half, hi, s] = jnp.concatenate([row[0:1, :w], row[0:1, w:], jnp.zeros((6, w), f32)], 0)
 
 
 def ffn(at, so, cotangent, mt, vec, wo, bi, bias_far, wi, wb, far):
@@ -379,7 +381,8 @@
     hidden = own * planes
     spec = lambda a, b: pl.BlockSpec((1, a, b), lambda i, *_: (i, 0, 0))
     st = lambda a, b, t: shape((spans, a, b), t)
-    half = (INNER // 2, planes, (width + own) // INNER + width // (planes * INNER) + 16, width)
+    half = (INNER // 2, planes, (width + own) // INNER + width // (planes * INNER), width)
+    side = (2, INNER // 2, planes, 8, width // 2)
     out = pl.BlockSpec(half, lambda i, *_: (0, 0, 0, 0), pipeline_mode=pl.Buffered(1))
     total = spans * pad
     vmem = pltpu.VMEM
@@ -390,7 +393,8 @@
             grid=(spans,),
             in_specs=[spec(pad, width), spec(rows, width), spec(width, lanes(pad))] + [whole(w) for w in (vec, wo, bi, bias_far)]
             + [ANY] * (2 + len(far)),
-            out_specs=[spec(rows, width), spec(pad, width), spec(pad, width), spec(width, lanes(pad)), out, out],
+            out_specs=[spec(rows, width), spec(pad, width), spec(pad, width), spec(width, lanes(pad)), out, out,
+                       pl.BlockSpec(side, lambda i, *_: (0,) * 5)],
             scratch_shapes=[vmem((8, 8, width), f32), vmem((8, hidden), f32), vmem((width, hidden), bf16), vmem((hidden, width), bf16),
                             vmem((pad, width), f32), vmem((pad, width), f32), vmem((pad, 128), f32),
                             vmem((total, hidden), bf16), vmem((total, hidden), bf16), vmem((total, width), bf16),
@@ -398,7 +402,8 @@
                             vmem((pad, width), bf16),
                             pltpu.SemaphoreType.DMA((2 + 2 * len(far) * (planes - 1),))],
         ),
-        out_shape=[st(rows, width, bf16), st(pad, width, f32), st(pad, width, bf16), st(width, lanes(pad), bf16)] + [shape(half, bf16)] * 2,
+        out_shape=[st(rows, width, bf16), st(pad, width, f32), st(pad, width, bf16), st(width, lanes(pad), bf16)] + [shape(half, bf16)] * 2
+        + [shape(side, f32)],
         compiler_params=params(62),
         cost_estimate=cost(46),
         name="ffn",
@@ -497,8 +502,8 @@
     )(*flat, *after)
 
 
-def back_body(rows, planes, group, skip, at_ref, x_ref, qt_ref, q_ref, k_ref, v_ref, mt_ref, dt_ref, d_ref, lt_ref, *refs):
-    dq_ref, dk_ref, dv_ref, o0_ref, o1_ref, aq, ak, av, ab, row, xp, vec, turn = refs[skip:]
+def back_body(rows, planes, group, skip, sides, at_ref, x_ref, qt_ref, q_ref, k_ref, v_ref, mt_ref, dt_ref, d_ref, lt_ref, *refs):
+    dq_ref, dk_ref, dv_ref, o0_ref, o1_ref, aq, ak, av, ab, row, xp, vec, turn = refs[sides + skip :]
     w, pad = k_ref.shape[2], k_ref.shape[1]
     width = x_ref.shape[-1]
     hs = width // HEADS
@@ -585,10 +590,12 @@
                         o_ref[hi, s, r : r + size, c : c + w] = turn[i, pl.ds(start, size), :].astype(bf16)
                     mine = vec[:, pl.ds(pl.multiple_of(plane * n, n), n)]
                     mine = jnp.concatenate([vector_rows(mine, at_ref[0] ^ peer, size), jnp.zeros((size, w - n), f32)], 1)
+                    if sides:
+                        mine = jnp.concatenate([mine[0:1], refs[0][half, hi, s, 0:2, :], mine[3:]], 0)
                     o_ref[hi, s, size:, w:] = mine.astype(bf16)
 
 
-def back(at, sequence, qt, q, k, v, mt, dt, d, lt, group, planes, after=()):
+def back(at, sequence, qt, q, k, v, mt, dt, d, lt, group, planes, sides=(), after=()):
     spans, rows, width = sequence.shape
     pad = k.shape[1]
     wide = qt.shape[2]
@@ -600,12 +607,13 @@
     half = (INNER // 2, planes, 2 * width // (planes * INNER), 2 * w)
     out = pl.BlockSpec(half, lambda i, *_: (0, 0, 0, 0))
     return pl.pallas_call(
-        functools.partial(back_body, rows, planes, group, len(after)),
+        functools.partial(back_body, rows, planes, group, len(after), len(sides)),
         grid_spec=pltpu.PrefetchScalarGridSpec(
             num_scalar_prefetch=1,
             grid=(spans,),
             in_specs=[pl.BlockSpec((1, rows, width), lambda i, *_: (i, 0, 0)), tr, nat, nat, nat, tr, tr, nat,
-                      pl.BlockSpec((1, 1, HEADS // GROUPS, wide), lambda i, *_: (i, group, 0, 0))] + [ANY] * len(after),
+                      pl.BlockSpec((1, 1, HEADS // GROUPS, wide), lambda i, *_: (i, group, 0, 0))] + [whole(a) for a in sides]
+            + [ANY] * len(after),
             out_specs=[grad, nat_grad, nat_grad] + [out] * 2,
             scratch_shapes=[pltpu.VMEM((w, width), f32)] * 3
             + [pltpu.VMEM((w, 8), f32), pltpu.VMEM((8, w), f32), pltpu.VMEM((pad, width), bf16), pltpu.VMEM((8, width), f32),
@@ -615,7 +623,7 @@
         compiler_params=params(),
         cost_estimate=cost(21),
         name=f"back{group}",
-    )(at, sequence, qt, q, k, v, mt, dt, d, lt, *after)
+    )(at, sequence, qt, q, k, v, mt, dt, d, lt, *sides, *after)
 
 
 def input_body(rows, groups, skip, *refs):
@@ -673,8 +681,8 @@
         at += cut_back
         wo_ref[small, :] = p[at : at + size, :].astype(f32)
         at += size
-        tail = p[at : at + 16, :].astype(f32)[0:1]
-        at += 16
+        tail = p[at + size : at + 2 * size, w : 2 * w].astype(f32)
+        tail = jnp.concatenate([tail[1:2], tail[2:3]], 1)
         pair = jnp.zeros((1, n), f32)
         for g in range(GROUPS):
             for i, o_ref in enumerate((wq_ref, wk_ref, wv_ref)):
@@ -752,11 +760,11 @@
     far, bias_far = join(far, first[:1])
     qt, k, v, mt, lt, so, q = attend(*common, head, spans - head, first, (far,))
     far = spread(far, (so,))
-    layer_out, gs, d, dt, keep, send = ffn(at, so, cotangent, mt, vec, w_out, b_in, bias_far, w_in, w_back, far)
-    *grad0, keep0, send0 = back(at, sequence, qt, q, k, v, mt, dt, d, lt, 0, planes)
+    layer_out, gs, d, dt, keep, send, side = ffn(at, so, cotangent, mt, vec, w_out, b_in, bias_far, w_in, w_back, far)
+    *grad0, keep0, send0 = back(at, sequence, qt, q, k, v, mt, dt, d, lt, 0, planes, (side,))
     got0 = swap(send0, 1)
     ffn_parts = core_sum([(keep, swap(send, 1))], (keep0,), "core_ffn")
-    *grad1, keep1, send1 = back(at, sequence, qt, q, k, v, mt, dt, d, lt, 1, planes, (ffn_parts[0], got0))
+    *grad1, keep1, send1 = back(at, sequence, qt, q, k, v, mt, dt, d, lt, 1, planes, (), (ffn_parts[0], got0))
     ffn_parts = from_plane(ffn_parts)
     parts = core_sum([(keep0, got0), (keep1, swap(send1, 1))], ffn_parts[1:], "core_attn")
     ffn_totals = to_planes(outer(plane_sum(ffn_parts, (parts[0],), "plane_ffn")))

time: 235 us -> 232 us (0.987)
  waiting for transfers between devices: 17.2 us -> 13.5 us
    ppermute x23, waiting for transfers between devices: 16.3 us -> 12.6 us  [swap(): return lax.ppermute(a, 'dp', [(i, i ^ k) for i in range(dp)])]
  transfers between devices with their start and end apart: 32 -> 32, of which waited for: 11 -> 10; matrix products, arithmetic and copies ran while one was open for 6% -> 6% of each run, Pallas kernels for 37% -> 38%
where the time goes in v2:
time: 232 us; the launch traced here: 228 us
  Pallas kernels  160 us (69%)
  starting transfers between devices  31.2 us (13%)
  local copies, waits for them, and re-layouts  21.7 us (9%)
  waiting for transfers between devices  13.5 us (6%)
    pallas_call x1, Pallas kernels, ffn(): pl.pallas_call(functools.partial(ffn_body, rows, len(far), planes), grid_...  59.2 us
    pallas_call x2, Pallas kernels, back(): pl.pallas_call(functools.partial(back_body, rows, planes, group, len(afte...  42.2 us
    pallas_call x2, Pallas kernels, attend(): pl.pallas_call(functools.partial(attend_body, rows, pad, len(before) + le...  24.8 us
    ppermute x23, starting transfers between devices, swap(): return lax.ppermute(a, 'dp', [(i, i ^ k) for i in range(dp)])  16.9 us
    ppermute x9, starting transfers between devices, turn(): return lax.ppermute(a, 'mp', [(i, (i + s) % planes) for i in range(planes)])  14.3 us
    ppermute x23, waiting for transfers between devices, swap(): return lax.ppermute(a, 'dp', [(i, i ^ k) for i in range(dp)])  12.6 us
    unnamed x78, local copies, waits for them, and re-layouts  12.2 us
    optimization_barrier x2, local copies, waits for them, and re-layouts, shards(): lax.optimization_barrier((layer_out, by_input, totals[0]))[:2]  9.58 us
  transfers between devices with their start and end apart: 32, of which 10 were waited for; matrix products, arithmetic and copies ran while one was open for 6% of the time, Pallas kernels for 38%

profile of v2, /device:TPU:0, one launch (start us, length us, event | category | flops | bytes accessed | tf_op | source)
XLA Modules:
  0.0 228.4 jit_solution(12413429649449446292)
XLA Ops:
  1.3 2.3 %prep.1.refs_8_ = bf16[144,512]{1,0:T(8,128)(2,1)} custom-call(s32[2]{0:T(128)} %pad_add_fusion.at_ref, bf16[512,512]{1,0:T(8,128)(2,1)} %wi_ref.3, bf16[512,512]{1,0:T(8,128)(2,1)} %wb_ref.3, bf16[512]{0:T(512)(128)(2,1)} %bi_ref.3), custom_call_target="tpu_custom_call" | custom-call | flops 2000000000 | bytes 200000 | tf_op jit(solution)/shard_map/prep/pallas_call | solution.py:79
  3.7 5.0 %collective-permute-start.2 = (bf16[144,512]{1,0:T(8,128)(2,1)}, bf16[144,512]{1,0:T(8,128)(2,1)S(1)}, u32[]{:S(2)}, u32[]{:S(2)}) collective-permute-start(bf16[144,512]{1,0:T(8,128)(2,1)} %prep.1.refs_8_), channel_id=1, source_target_pairs={{0,3},{1,0},{2,1},{3,2},{4,7},{5,4},{6,5},{7,6},{8,11},{9,8},{10,9... | collective-permute-start | bytes 442376 | tf_op jit(solution)/shard_map/ppermute | solution.py:733
  12.9 7.6 %attend0.1 = (bf16[4,512,640]{2,1,0:T(8,128)(2,1)}, bf16[4,544,512]{2,1,0:T(8,128)(2,1)}, bf16[4,544,512]{2,1,0:T(8,128)(2,1)}, bf16[4,512,640]{2,1,0:T(8,128)(2...) custom-call(bf16[4,532,512]{2,1,0:T(8,128)(2,1)} %copy.42.x_ref, ...), custom_call_target="tpu_custom_call" | custom-call | flops 16000000000 | bytes 1600000 | tf_op jit(solution)/shard_map/attend0/pallas_call | solution.py:179
  22.1 1.8 join.1
  23.9 2.4 %collective-permute-start.5 = (bf16[3,128,512]{2,1,0:T(8,128)(2,1)}, bf16[3,128,512]{2,1,0:T(8,128)(2,1)S(1)}, u32[]{:S(2)}, u32[]{:S(2)}) collective-permute-start(bf16[3,128,512]{2,1,0:T(8,128)(2,1)} %get-tuple-element.102.refs_7_.refs_0_), channel_id=1, source_target_pairs={{0,24},{4,28},{8,16},{12,20},{16,8},{20,12},{24,0},{28,4},{1,25},{... | collective-permute-start | bytes 1179656 | tf_op jit(solution)/shard_map/ppermute | solution.py:730
  27.4 17.2 %attend1.1 = (bf16[4,512,640]{2,1,0:T(8,128)(2,1)}, bf16[4,544,512]{2,1,0:T(8,128)(2,1)}, bf16[4,544,512]{2,1,0:T(8,128)(2,1)}, bf16[4,512,640]{2,1,0:T(8,128)(2...) custom-call(bf16[4,532,512]{2,1,0:T(8,128)(2,1)} %copy.42.x_ref, ...), custom_call_target="tpu_custom_call", output_to_operand_aliasing={{0}: (6, {}), {1}: (7, {}), {2}: (8, {}), {3}: (9, {}), {4}... | custom-call | flops 16000000000 | bytes 1600000 | tf_op jit(solution)/shard_map/attend1/pallas_call | solution.py:179
  49.1 59.2 %ffn.1 = (bf16[4,532,512]{2,1,0:T(8,128)(2,1)}, f32[4,544,512]{2,1,0:T(8,128)}, bf16[4,544,512]{2,1,0:T(8,128)(2,1)}, bf16[4,512,640]{2,1,0:T(8,128)(2,1)}, bf16...) custom-call(s32[2]{0:T(128)} %pad_add_fusion.at_ref, ...), custom_call_target="tpu_custom_call" | custom-call | flops 46000001024 | bytes 4600000 | tf_op jit(solution)/shard_map/ffn/pallas_call | solution.py:389
  108.5 21.4 %back0.1 = (bf16[4,256,640]{2,1,0:T(8,128)(2,1)}, bf16[4,544,256]{2,1,0:T(8,128)(2,1)}, bf16[4,544,256]{2,1,0:T(8,128)(2,1)}, bf16[4,4,32,512]{3,2,1,0:T(8,128)(2,1)}, bf16[4,4,32,512]{3,2,1,0:T(8,128)(2,1)}) custom-call(s32[2]{0:T(128)} %pad_add_fusion.at_ref, bf16[4,532,512]{2,1,0:T(8,128)(2,1)} %copy.42.x_ref, ...), custom_call_target="tpu_custom_call" | custom-call | flops 20999999488 | bytes 2100000 | tf_op jit(solution)/shard_map/back0/pallas_call | solution.py:609
  131.9 4.3 %core_ffn.1 = (bf16[4,144,512]{2,1,0:T(8,128)(2,1)}, bf16[4,144,512]{2,1,0:T(8,128)(2,1)}, bf16[4,144,512]{2,1,0:T(8,128)(2,1)}, bf16[4,144,512]{2,1,0:T(8,128)(2,1)}) custom-call(bf16[4,4,144,512]{3,2,1,0:T(8,128)(2,1)} %get-tuple-element.107.refs_0_, bf16[4,4,144,512]{3,2,1,0:T(8,128)(2,1)} %copy-done, ...), custom_call_target="tpu_custom_call" | custom-call | flops 1000000 | bytes 100 | tf_op jit(solution)/shard_map/core_ffn/pallas_call | solution.py:451
  140.5 20.8 %back1.1 = (bf16[4,256,640]{2,1,0:T(8,128)(2,1)}, bf16[4,544,256]{2,1,0:T(8,128)(2,1)}, bf16[4,544,256]{2,1,0:T(8,128)(2,1)}, bf16[4,4,32,512]{3,2,1,0:T(8,128)(2,1)}, bf16[4,4,32,512]{3,2,1,0:T(8,128)(2,1)}) custom-call(s32[2]{0:T(128)} %pad_add_fusion.at_ref, bf16[4,532,512]{2,1,0:T(8,128)(2,1)} %copy.42.x_ref, ...), custom_call_target="tpu_custom_call" | custom-call | flops 20999999488 | bytes 2100000 | tf_op jit(solution)/shard_map/back1/pallas_call | solution.py:609
  161.3 2.1 collective-permute-done.15.refs_3_
  163.5 2.1 collective-permute-done.12.refs_5_.refs_2_
  166.5 3.6 %core_attn.1 = (bf16[4,64,512]{2,1,0:T(8,128)(2,1)}, bf16[4,64,512]{2,1,0:T(8,128)(2,1)}, bf16[4,64,512]{2,1,0:T(8,128)(2,1)}, bf16[4,64,512]{2,1,0:T(8,128)(2,1)}) custom-call(bf16[4,4,32,512]{3,2,1,0:T(8,128)(2,1)} %get-tuple-element.117.refs_2_.refs_0_, bf16[4,4,32,512]{3,2,1,0:T(8,128)(2,1)} %copy-done.7, ...), custom_call_target="tpu_custom_call" | custom-call | flops 1000000 | bytes 100 | tf_op jit(solution)/shard_map/core_attn/pallas_call | solution.py:451
  171.2 2.5 %plane_ffn.1 = (bf16[144,512]{1,0:T(8,128)(2,1)}, bf16[144,512]{1,0:T(8,128)(2,1)}, bf16[144,512]{1,0:T(8,128)(2,1)}, bf16[144,512]{1,0:T(8,128)(2,1)}) custom-call(bf16[4,144,512]{2,1,0:T(8,128)(2,1)} %get-tuple-element.118.refs_0_, bf16[4,144,512]{2,1,0:T(8,128)(2,1)} %copy-done.1, bf16[4,144,512]{2,1,0:T(8,128)(2,1)} %copy-done.2, ...), custom_call_target="tpu_custom_call" | custom-call | flops 1000000 | bytes 100 | tf_op jit(solution)/shard_map/plane_ffn/pallas_call | solution.py:471
  173.7 2.0 collective-permute-start.19
  181.1 9.5 %input_grad.1.refs_4_ = f32[4,532,512]{2,1,0:T(8,128)} custom-call(bf16[144,512]{1,0:T(8,128)(2,1)} %get-tuple-element.126.refs_0_, f32[4,544,512]{2,1,0:T(8,128)} %get-tuple-element.127.refs_1_, bf16[4,256,640]{2,1,0:T(8,128)(2,1)} %get-tuple-element.128.refs_2_, bf16[4,544,256]{2,1,0:T(8,128)(2,1)} %get-tuple-element.129.refs_3_, ...), custom_call_target="tpu_custom_call" | custom-call | flops 10000000000 | bytes 1000000 | tf_op jit(solution)/shard_map/input_grad/pallas_call | solution.py:655
  192.0 1.9 plane_attn.1
  194.0 2.1 collective-permute-start.22
  197.4 2.5 %copy.51 = bf16[4,532,512]{2,0,1:T(4,128)(2,1)} copy(bf16[4,532,512]{2,1,0:T(8,128)(2,1)S(1)} %copy-done.4) | data formatting | bytes 4358144 | tf_op jit(solution)/shard_map/optimization_barrier | solution.py:773
  199.8 7.1 %copy.50 = f32[4,532,512]{2,0,1:T(4,128)} copy(f32[4,532,512]{2,1,0:T(8,128)} %input_grad.1.refs_4_) | data formatting | bytes 8716288 | tf_op jit(solution)/shard_map/optimization_barrier | solution.py:773
  208.3 2.0 last.1.refs_0_
  213.8 4.6 %collective-permute-done.27.refs_3_ = bf16[208,512]{1,0:T(8,128)(2,1)S(1)} collective-permute-done((bf16[208,512]{1,0:T(8,128)(2,1)}, bf16[208,512]{1,0:T(8,128)(2,1)S(1)}, u32[]{:S(2)}, u32[]{:S(2)}) %collective-permute-start.27) | collective-permute-done | bytes 213024 | tf_op jit(solution)/shard_map/ppermute | solution.py:730
  218.4 1.8 collective-permute-done.26.refs_2_
  223.8 4.4 %final.1 = (f32[512,512]{1,0:T(8,128)}, f32[512,512]{1,0:T(8,128)}, f32[128,512]{1,0:T(8,128)}, f32[128,512]{1,0:T(8,128)}, f32[128,512]{1,0:T(8,128)}, /*index=...) custom-call(s32[2]{0:T(128)} %pad_add_fusion.at_ref, ...), custom_call_target="tpu_custom_call" | custom-call | flops 3000000000 | bytes 300000 | tf_op jit(solution)/shard_map/final/pallas_call | solution.py:708
  (136 shorter events, 36.7 us)
Async XLA Ops:
  3.7 16.8 %collective-permute-start.2 = (bf16[144,512]{1,0:T(8,128)(2,1)}, bf16[144,512]{1,0:T(8,128)(2,1)S(1)}, u32[]{:S(2)}, u32[]{:S(2)}) collective-permute-start(bf16[144,512]{1,0:T(8,128)(2,1)} %prep.1.refs_8_), channel_id=1, source_target_pairs={{0,3},{1,0},{2,1},{3,2},{4,7},{5,4},{6,5},{7,6},{8,11},{9,8},{10,9... | collective-permute-start | bytes 442376 | tf_op jit(solution)/shard_map/ppermute | solution.py:733
  8.7 12.7 %collective-permute-start.1 = (bf16[144,512]{1,0:T(8,128)(2,1)}, bf16[144,512]{1,0:T(8,128)(2,1)S(1)}, u32[]{:S(2)}, u32[]{:S(2)}) collective-permute-start(bf16[144,512]{1,0:T(8,128)(2,1)} %prep.1.refs_8_), channel_id=1, source_target_pairs={{0,2},{1,3},{2,0},{3,1},{4,6},{5,7},{6,4},{7,5},{8,10},{9,11},{10,... | collective-permute-start | bytes 442376 | tf_op jit(solution)/shard_map/ppermute | solution.py:733
  8.7 12.7 %collective-permute-start = (bf16[144,512]{1,0:T(8,128)(2,1)}, bf16[144,512]{1,0:T(8,128)(2,1)S(1)}, u32[]{:S(2)}, u32[]{:S(2)}) collective-permute-start(bf16[144,512]{1,0:T(8,128)(2,1)} %prep.1.refs_8_), channel_id=1, source_target_pairs={{0,1},{1,2},{2,3},{3,0},{4,5},{5,6},{6,7},{7,4},{8,9},{9,10},{10,1... | collective-permute-start | bytes 442376 | tf_op jit(solution)/shard_map/ppermute | solution.py:733
  23.9 20.7 %collective-permute-start.5 = (bf16[3,128,512]{2,1,0:T(8,128)(2,1)}, bf16[3,128,512]{2,1,0:T(8,128)(2,1)S(1)}, u32[]{:S(2)}, u32[]{:S(2)}) collective-permute-start(bf16[3,128,512]{2,1,0:T(8,128)(2,1)} %get-tuple-element.102.refs_7_.refs_0_), channel_id=1, source_target_pairs={{0,24},{4,28},{8,16},{12,20},{16,8},{20,12},{24,0},{28,4},{1,25},{... | collective-permute-start | bytes 1179656 | tf_op jit(solution)/shard_map/ppermute | solution.py:730
  26.4 18.3 %collective-permute-start.4 = (bf16[3,128,512]{2,1,0:T(8,128)(2,1)}, bf16[3,128,512]{2,1,0:T(8,128)(2,1)S(1)}, u32[]{:S(2)}, u32[]{:S(2)}) collective-permute-start(bf16[3,128,512]{2,1,0:T(8,128)(2,1)} %get-tuple-element.102.refs_7_.refs_0_), channel_id=1, source_target_pairs={{0,16},{4,20},{8,24},{12,28},{16,0},{20,4},{24,8},{28,12},{1,17},{... | collective-permute-start | bytes 1179656 | tf_op jit(solution)/shard_map/ppermute | solution.py:730
  26.9 17.8 %collective-permute-start.3 = (bf16[3,128,512]{2,1,0:T(8,128)(2,1)}, bf16[3,128,512]{2,1,0:T(8,128)(2,1)S(1)}, u32[]{:S(2)}, u32[]{:S(2)}) collective-permute-start(bf16[3,128,512]{2,1,0:T(8,128)(2,1)} %get-tuple-element.102.refs_7_.refs_0_), channel_id=1, source_target_pairs={{0,8},{4,12},{8,0},{12,4},{16,24},{20,28},{24,16},{28,20},{1,9},{5... | collective-permute-start | bytes 1179656 | tf_op jit(solution)/shard_map/ppermute | solution.py:730
  44.8 2.9 %collective-permute-start.6 = (bf16[3,128,512]{2,1,0:T(8,128)(2,1)S(1)}, bf16[3,128,512]{2,1,0:T(8,128)(2,1)S(1)}, u32[]{:S(2)}, u32[]{:S(2)}) collective-permute-start(bf16[3,128,512]{2,1,0:T(8,128)(2,1)S(1)} %copy-done.18), channel_id=1, source_target_pairs={{0,4},{4,0},{8,12},{12,8},{16,20},{20,16},{24,28},{28,24},{1,5},{5... | collective-permute-start | bytes 1179656 | tf_op jit(solution)/shard_map/ppermute | solution.py:730
  108.4 22.1 %collective-permute-start.10 = (bf16[4,4,144,512]{3,2,1,0:T(8,128)(2,1)}, bf16[4,4,144,512]{3,2,1,0:T(8,128)(2,1)S(1)}, u32[]{:S(2)}, u32[]{:S(2)}) collective-permute-start(bf16[4,4,144,512]{3,2,1,0:T(8,128)(2,1)} %get-tuple-element.108), channel_id=1, source_target_pairs={{0,4},{4,0},{8,12},{12,8},{16,20},{20,16},{24,28},{28,24},{1,5},{5... | collective-permute-start | bytes 7077896 | tf_op jit(solution)/shard_map/ppermute | solution.py:730
  130.0 9.7 %collective-permute-start.14 = (bf16[4,4,32,512]{3,2,1,0:T(8,128)(2,1)}, bf16[4,4,32,512]{3,2,1,0:T(8,128)(2,1)S(1)}, u32[]{:S(2)}, u32[]{:S(2)}) collective-permute-start(bf16[4,4,32,512]{3,2,1,0:T(8,128)(2,1)} %get-tuple-element.122), channel_id=1, source_target_pairs={{0,4},{4,0},{8,12},{12,8},{16,20},{20,16},{24,28},{28,24},{1,5},{5... | collective-permute-start | bytes 1572872 | tf_op jit(solution)/shard_map/ppermute | solution.py:730
  136.1 27.3 %collective-permute-start.11 = (bf16[4,144,512]{2,1,0:T(8,128)(2,1)}, bf16[4,144,512]{2,1,0:T(8,128)(2,1)S(1)}, u32[]{:S(2)}, u32[]{:S(2)}) collective-permute-start(bf16[4,144,512]{2,1,0:T(8,128)(2,1)} %get-tuple-element.119), channel_id=1, source_target_pairs={{0,8},{4,12},{8,0},{12,4},{16,24},{20,28},{24,16},{28,20},{1,9},{5... | collective-permute-start | bytes 1769480 | tf_op jit(solution)/shard_map/ppermute | solution.py:730
  137.6 27.9 %collective-permute-start.12 = (bf16[4,144,512]{2,1,0:T(8,128)(2,1)}, bf16[4,144,512]{2,1,0:T(8,128)(2,1)S(1)}, u32[]{:S(2)}, u32[]{:S(2)}) collective-permute-start(bf16[4,144,512]{2,1,0:T(8,128)(2,1)} %get-tuple-element.120), channel_id=1, source_target_pairs={{0,16},{4,20},{8,24},{12,28},{16,0},{20,4},{24,8},{28,12},{1,17},{... | collective-permute-start | bytes 1769480 | tf_op jit(solution)/shard_map/ppermute | solution.py:730
  139.1 26.4 %collective-permute-start.13 = (bf16[4,144,512]{2,1,0:T(8,128)(2,1)}, bf16[4,144,512]{2,1,0:T(8,128)(2,1)S(1)}, u32[]{:S(2)}, u32[]{:S(2)}) collective-permute-start(bf16[4,144,512]{2,1,0:T(8,128)(2,1)} %get-tuple-element.121), channel_id=1, source_target_pairs={{0,24},{4,28},{8,16},{12,20},{16,8},{20,12},{24,0},{28,4},{1,25},{... | collective-permute-start | bytes 1769480 | tf_op jit(solution)/shard_map/ppermute | solution.py:730
  170.1 9.4 %collective-permute-start.16 = (bf16[4,64,512]{2,1,0:T(8,128)(2,1)}, bf16[4,64,512]{2,1,0:T(8,128)(2,1)S(1)}, u32[]{:S(2)}, u32[]{:S(2)}) collective-permute-start(bf16[4,64,512]{2,1,0:T(8,128)(2,1)} %get-tuple-element.134), channel_id=1, source_target_pairs={{0,8},{4,12},{8,0},{12,4},{16,24},{20,28},{24,16},{28,20},{1,9},{5... | collective-permute-start | bytes 786440 | tf_op jit(solution)/shard_map/ppermute | solution.py:730
  173.7 22.4 %collective-permute-start.19 = (bf16[144,512]{1,0:T(8,128)(2,1)}, bf16[144,512]{1,0:T(8,128)(2,1)S(1)}, u32[]{:S(2)}, u32[]{:S(2)}) collective-permute-start(bf16[144,512]{1,0:T(8,128)(2,1)} %get-tuple-element.140), channel_id=1, source_target_pairs={{0,3},{1,0},{2,1},{3,2},{4,7},{5,4},{6,5},{7,6},{8,11},{9,8},{10,9... | collective-permute-start | bytes 442376 | tf_op jit(solution)/shard_map/ppermute | solution.py:733
  175.7 31.2 %collective-permute-start.20 = (bf16[144,512]{1,0:T(8,128)(2,1)}, bf16[144,512]{1,0:T(8,128)(2,1)S(1)}, u32[]{:S(2)}, u32[]{:S(2)}) collective-permute-start(bf16[144,512]{1,0:T(8,128)(2,1)} %get-tuple-element.141), channel_id=1, source_target_pairs={{0,2},{1,3},{2,0},{3,1},{4,6},{5,7},{6,4},{7,5},{8,10},{9,11},{10,... | collective-permute-start | bytes 442376 | tf_op jit(solution)/shard_map/ppermute | solution.py:733
  176.9 30.1 %collective-permute-start.21 = (bf16[144,512]{1,0:T(8,128)(2,1)}, bf16[144,512]{1,0:T(8,128)(2,1)S(1)}, u32[]{:S(2)}, u32[]{:S(2)}) collective-permute-start(bf16[144,512]{1,0:T(8,128)(2,1)} %get-tuple-element.142), channel_id=1, source_target_pairs={{0,1},{1,2},{2,3},{3,0},{4,5},{5,6},{6,7},{7,4},{8,9},{9,10},{10,1... | collective-permute-start | bytes 442376 | tf_op jit(solution)/shard_map/ppermute | solution.py:733
  178.6 12.1 %collective-permute-start.17 = (bf16[4,64,512]{2,1,0:T(8,128)(2,1)S(1)}, bf16[4,64,512]{2,1,0:T(8,128)(2,1)S(1)}, u32[]{:S(2)}, u32[]{:S(2)}) collective-permute-start(bf16[4,64,512]{2,1,0:T(8,128)(2,1)S(1)} %copy-done.27), channel_id=1, source_target_pairs={{0,16},{4,20},{8,24},{12,28},{16,0},{20,4},{24,8},{28,12},{1,17},{... | collective-permute-start | bytes 786440 | tf_op jit(solution)/shard_map/ppermute | solution.py:730
  179.5 11.1 %collective-permute-start.18 = (bf16[4,64,512]{2,1,0:T(8,128)(2,1)S(1)}, bf16[4,64,512]{2,1,0:T(8,128)(2,1)S(1)}, u32[]{:S(2)}, u32[]{:S(2)}) collective-permute-start(bf16[4,64,512]{2,1,0:T(8,128)(2,1)S(1)} %copy-done.26), channel_id=1, source_target_pairs={{0,24},{4,28},{8,16},{12,20},{16,8},{20,12},{24,0},{28,4},{1,25},{... | collective-permute-start | bytes 786440 | tf_op jit(solution)/shard_map/ppermute | solution.py:730
  194.0 13.0 %collective-permute-start.22 = (bf16[64,512]{1,0:T(8,128)(2,1)}, bf16[64,512]{1,0:T(8,128)(2,1)S(1)}, u32[]{:S(2)}, u32[]{:S(2)}) collective-permute-start(bf16[64,512]{1,0:T(8,128)(2,1)} %get-tuple-element.143), channel_id=1, source_target_pairs={{0,3},{1,0},{2,1},{3,2},{4,7},{5,4},{6,5},{7,6},{8,11},{9,8},{10,9... | collective-permute-start | bytes 196616 | tf_op jit(solution)/shard_map/ppermute | solution.py:733
  196.1 10.9 %collective-permute-start.23 = (bf16[64,512]{1,0:T(8,128)(2,1)}, bf16[64,512]{1,0:T(8,128)(2,1)S(1)}, u32[]{:S(2)}, u32[]{:S(2)}) collective-permute-start(bf16[64,512]{1,0:T(8,128)(2,1)} %get-tuple-element.144), channel_id=1, source_target_pairs={{0,2},{1,3},{2,0},{3,1},{4,6},{5,7},{6,4},{7,5},{8,10},{9,11},{10,... | collective-permute-start | bytes 196616 | tf_op jit(solution)/shard_map/ppermute | solution.py:733
  196.1 10.9 %collective-permute-start.24 = (bf16[64,512]{1,0:T(8,128)(2,1)}, bf16[64,512]{1,0:T(8,128)(2,1)S(1)}, u32[]{:S(2)}, u32[]{:S(2)}) collective-permute-start(bf16[64,512]{1,0:T(8,128)(2,1)} %get-tuple-element.145), channel_id=1, source_target_pairs={{0,1},{1,2},{2,3},{3,0},{4,5},{5,6},{6,7},{7,4},{8,9},{9,10},{10,1... | collective-permute-start | bytes 196616 | tf_op jit(solution)/shard_map/ppermute | solution.py:733
  210.3 8.1 %collective-permute-start.27 = (bf16[208,512]{1,0:T(8,128)(2,1)}, bf16[208,512]{1,0:T(8,128)(2,1)S(1)}, u32[]{:S(2)}, u32[]{:S(2)}) collective-permute-start(bf16[208,512]{1,0:T(8,128)(2,1)} %last.1.refs_0_), channel_id=1, source_target_pairs={{0,24},{4,28},{8,16},{12,20},{16,8},{20,12},{24,0},{28,4},{1,25},{... | collective-permute-start | bytes 638984 | tf_op jit(solution)/shard_map/ppermute | solution.py:730
  211.3 9.0 %collective-permute-start.26 = (bf16[208,512]{1,0:T(8,128)(2,1)}, bf16[208,512]{1,0:T(8,128)(2,1)S(1)}, u32[]{:S(2)}, u32[]{:S(2)}) collective-permute-start(bf16[208,512]{1,0:T(8,128)(2,1)} %last.1.refs_0_), channel_id=1, source_target_pairs={{0,16},{4,20},{8,24},{12,28},{16,0},{20,4},{24,8},{28,12},{1,17},{... | collective-permute-start | bytes 638984 | tf_op jit(solution)/shard_map/ppermute | solution.py:730
  212.3 8.0 %collective-permute-start.25 = (bf16[208,512]{1,0:T(8,128)(2,1)}, bf16[208,512]{1,0:T(8,128)(2,1)S(1)}, u32[]{:S(2)}, u32[]{:S(2)}) collective-permute-start(bf16[208,512]{1,0:T(8,128)(2,1)} %last.1.refs_0_), channel_id=1, source_target_pairs={{0,8},{4,12},{8,0},{12,4},{16,24},{20,28},{24,16},{28,20},{1,9},{5... | collective-permute-start | bytes 638984 | tf_op jit(solution)/shard_map/ppermute | solution.py:730
  (46 other events, 151.5 us)

commit v3 on v2

--- a/solution.py
+++ b/solution.py
@@ -766,13 +766,15 @@
     ffn_parts = core_sum([(keep, swap(send, 1))], (keep0,), "core_ffn")
     *grad1, keep1, send1 = back(at, sequence, qt, q, k, v, mt, dt, d, lt, 1, planes, (), (ffn_parts[0], got0))
     ffn_parts = from_plane(ffn_parts)
-    parts = core_sum([(keep0, got0), (keep1, swap(send1, 1))], ffn_parts[1:], "core_attn")
+    layer_out = lax.optimization_barrier((layer_out, keep1))[0]
+    layer_out = lax.optimization_barrier(jnp.transpose(layer_out, (1, 0, 2)))
+    parts = core_sum([(keep0, got0), (keep1, swap(send1, 1))], (*ffn_parts[1:], layer_out), "core_attn")
     ffn_totals = to_planes(outer(plane_sum(ffn_parts, (parts[0],), "plane_ffn")))
     by_input = input_grad(rows, gs, [grad0, grad1], w_query, w_key, w_value, (ffn_totals[0],))
     totals = to_planes(outer(plane_sum(from_plane(parts), (by_input,), "plane_attn")))
-    layer_out, by_input = lax.optimization_barrier((layer_out, by_input, totals[0]))[:2]
-    layer_out, by_input = (lax.optimization_barrier(jnp.transpose(a, (1, 0, 2))) for a in (layer_out, by_input))
-    pieces = spread(last_sum([ffn_totals, totals], (by_input, layer_out), "last"))
+    by_input = lax.optimization_barrier((by_input, totals[0]))[0]
+    by_input = lax.optimization_barrier(jnp.transpose(by_input, (1, 0, 2)))
+    pieces = spread(last_sum([ffn_totals, totals], (by_input,), "last"))
     wi, wb, wo, wq, wk, wv, bins, gg2, gs2, bb, gg1, gs1, bo, bq, bv = final(at, pieces, own, planes)
     row = lambda a: a.reshape(-1)
     layer_out, by_input = (jnp.transpose(a, (1, 0, 2)) for a in (layer_out, by_input))

time: 232 us -> 232 us (level)
  no operation moved by 1% of the time
where the time goes in v3:
time: 232 us; the launch traced here: 228 us
  Pallas kernels  160 us (69%)
  starting transfers between devices  31.7 us (14%)
  local copies, waits for them, and re-layouts  22.4 us (10%)
  waiting for transfers between devices  12.1 us (5%)
    pallas_call x1, Pallas kernels, ffn(): pl.pallas_call(functools.partial(ffn_body, rows, len(far), planes), grid_...  59.2 us
    pallas_call x2, Pallas kernels, back(): pl.pallas_call(functools.partial(back_body, rows, planes, group, len(afte...  42.3 us
    pallas_call x2, Pallas kernels, attend(): pl.pallas_call(functools.partial(attend_body, rows, pad, len(before) + le...  24.8 us
    ppermute x23, starting transfers between devices, swap(): return lax.ppermute(a, 'dp', [(i, i ^ k) for i in range(dp)])  16.9 us
    ppermute x9, starting transfers between devices, turn(): return lax.ppermute(a, 'mp', [(i, (i + s) % planes) for i in range(planes)])  14.7 us
    unnamed x78, local copies, waits for them, and re-layouts  12.8 us
    ppermute x23, waiting for transfers between devices, swap(): return lax.ppermute(a, 'dp', [(i, i ^ k) for i in range(dp)])  11.2 us
    pallas_call x1, Pallas kernels, input_grad(): pl.pallas_call(functools.partial(input_body, rows, len(parts), len(after)...  9.76 us
  transfers between devices with their start and end apart: 32, of which 10 were waited for; matrix products, arithmetic and copies ran while one was open for 6% of the time, Pallas kernels for 38%

profile of v3, /device:TPU:0, one launch (start us, length us, event | category | flops | bytes accessed | tf_op | source)
XLA Modules:
  0.0 228.4 jit_solution(9712325017872528134)
XLA Ops:
  1.3 2.3 %prep.1.refs_8_ = bf16[144,512]{1,0:T(8,128)(2,1)} custom-call(s32[2]{0:T(128)} %pad_add_fusion.at_ref, bf16[512,512]{1,0:T(8,128)(2,1)} %wi_ref.3, bf16[512,512]{1,0:T(8,128)(2,1)} %wb_ref.3, bf16[512]{0:T(512)(128)(2,1)} %bi_ref.3), custom_call_target="tpu_custom_call" | custom-call | flops 2000000000 | bytes 200000 | tf_op jit(solution)/shard_map/prep/pallas_call | solution.py:79
  3.7 5.0 %collective-permute-start.2 = (bf16[144,512]{1,0:T(8,128)(2,1)}, bf16[144,512]{1,0:T(8,128)(2,1)S(1)}, u32[]{:S(2)}, u32[]{:S(2)}) collective-permute-start(bf16[144,512]{1,0:T(8,128)(2,1)} %prep.1.refs_8_), channel_id=1, source_target_pairs={{0,3},{1,0},{2,1},{3,2},{4,7},{5,4},{6,5},{7,6},{8,11},{9,8},{10,9... | collective-permute-start | bytes 442376 | tf_op jit(solution)/shard_map/ppermute | solution.py:733
  9.7 1.8 copy.42.x_ref
  13.0 7.6 %attend0.1 = (bf16[4,512,640]{2,1,0:T(8,128)(2,1)}, bf16[4,544,512]{2,1,0:T(8,128)(2,1)}, bf16[4,544,512]{2,1,0:T(8,128)(2,1)}, bf16[4,512,640]{2,1,0:T(8,128)(2...) custom-call(bf16[4,532,512]{2,1,0:T(8,128)(2,1)} %copy.42.x_ref, ...), custom_call_target="tpu_custom_call" | custom-call | flops 16000000000 | bytes 1600000 | tf_op jit(solution)/shard_map/attend0/pallas_call | solution.py:179
  22.1 1.8 join.1
  23.9 2.4 %collective-permute-start.5 = (bf16[3,128,512]{2,1,0:T(8,128)(2,1)}, bf16[3,128,512]{2,1,0:T(8,128)(2,1)S(1)}, u32[]{:S(2)}, u32[]{:S(2)}) collective-permute-start(bf16[3,128,512]{2,1,0:T(8,128)(2,1)} %get-tuple-element.102.refs_7_.refs_0_), channel_id=1, source_target_pairs={{0,24},{4,28},{8,16},{12,20},{16,8},{20,12},{24,0},{28,4},{1,25},{... | collective-permute-start | bytes 1179656 | tf_op jit(solution)/shard_map/ppermute | solution.py:730
  27.4 17.2 %attend1.1 = (bf16[4,512,640]{2,1,0:T(8,128)(2,1)}, bf16[4,544,512]{2,1,0:T(8,128)(2,1)}, bf16[4,544,512]{2,1,0:T(8,128)(2,1)}, bf16[4,512,640]{2,1,0:T(8,128)(2...) custom-call(bf16[4,532,512]{2,1,0:T(8,128)(2,1)} %copy.42.x_ref, ...), custom_call_target="tpu_custom_call", output_to_operand_aliasing={{0}: (6, {}), {1}: (7, {}), {2}: (8, {}), {3}: (9, {}), {4}... | custom-call | flops 16000000000 | bytes 1600000 | tf_op jit(solution)/shard_map/attend1/pallas_call | solution.py:179
  45.8 1.8 copy.43.ct_ref
  49.1 59.2 %ffn.1 = (bf16[4,532,512]{2,1,0:T(8,128)(2,1)}, f32[4,544,512]{2,1,0:T(8,128)}, bf16[4,544,512]{2,1,0:T(8,128)(2,1)}, bf16[4,512,640]{2,1,0:T(8,128)(2,1)}, bf16...) custom-call(s32[2]{0:T(128)} %pad_add_fusion.at_ref, ...), custom_call_target="tpu_custom_call" | custom-call | flops 46000001024 | bytes 4600000 | tf_op jit(solution)/shard_map/ffn/pallas_call | solution.py:389
  108.5 21.4 %back0.1 = (bf16[4,256,640]{2,1,0:T(8,128)(2,1)}, bf16[4,544,256]{2,1,0:T(8,128)(2,1)}, bf16[4,544,256]{2,1,0:T(8,128)(2,1)}, bf16[4,4,32,512]{3,2,1,0:T(8,128)(2,1)}, bf16[4,4,32,512]{3,2,1,0:T(8,128)(2,1)}) custom-call(s32[2]{0:T(128)} %pad_add_fusion.at_ref, bf16[4,532,512]{2,1,0:T(8,128)(2,1)} %copy.42.x_ref, ...), custom_call_target="tpu_custom_call" | custom-call | flops 20999999488 | bytes 2100000 | tf_op jit(solution)/shard_map/back0/pallas_call | solution.py:609
  131.8 4.3 %core_ffn.1 = (bf16[4,144,512]{2,1,0:T(8,128)(2,1)}, bf16[4,144,512]{2,1,0:T(8,128)(2,1)}, bf16[4,144,512]{2,1,0:T(8,128)(2,1)}, bf16[4,144,512]{2,1,0:T(8,128)(2,1)}) custom-call(bf16[4,4,144,512]{3,2,1,0:T(8,128)(2,1)} %get-tuple-element.114.refs_0_, bf16[4,4,144,512]{3,2,1,0:T(8,128)(2,1)} %copy-done.3, ...), custom_call_target="tpu_custom_call" | custom-call | flops 1000000 | bytes 100 | tf_op jit(solution)/shard_map/core_ffn/pallas_call | solution.py:451
  140.4 20.9 %back1.1 = (bf16[4,256,640]{2,1,0:T(8,128)(2,1)}, bf16[4,544,256]{2,1,0:T(8,128)(2,1)}, bf16[4,544,256]{2,1,0:T(8,128)(2,1)}, bf16[4,4,32,512]{3,2,1,0:T(8,128)(2,1)}, bf16[4,4,32,512]{3,2,1,0:T(8,128)(2,1)}) custom-call(s32[2]{0:T(128)} %pad_add_fusion.at_ref, bf16[4,532,512]{2,1,0:T(8,128)(2,1)} %copy.42.x_ref, ...), custom_call_target="tpu_custom_call" | custom-call | flops 20999999488 | bytes 2100000 | tf_op jit(solution)/shard_map/back1/pallas_call | solution.py:609
  161.4 2.5 %copy.51 = bf16[4,532,512]{2,0,1:T(4,128)(2,1)} copy(bf16[4,532,512]{2,1,0:T(8,128)(2,1)S(1)} %copy-done.4) | data formatting | bytes 4358144 | tf_op jit(solution)/shard_map/optimization_barrier | solution.py:769
  167.1 3.6 %core_attn.1 = (bf16[4,64,512]{2,1,0:T(8,128)(2,1)}, bf16[4,64,512]{2,1,0:T(8,128)(2,1)}, bf16[4,64,512]{2,1,0:T(8,128)(2,1)}, bf16[4,64,512]{2,1,0:T(8,128)(2,1)}) custom-call(bf16[4,4,32,512]{3,2,1,0:T(8,128)(2,1)} %get-tuple-element.117.refs_2_.refs_0_, bf16[4,4,32,512]{3,2,1,0:T(8,128)(2,1)} %copy-done.7, ...), custom_call_target="tpu_custom_call" | custom-call | flops 1000000 | bytes 100 | tf_op jit(solution)/shard_map/core_attn/pallas_call | solution.py:451
  171.5 2.5 %plane_ffn.1 = (bf16[144,512]{1,0:T(8,128)(2,1)}, bf16[144,512]{1,0:T(8,128)(2,1)}, bf16[144,512]{1,0:T(8,128)(2,1)}, bf16[144,512]{1,0:T(8,128)(2,1)}) custom-call(bf16[4,144,512]{2,1,0:T(8,128)(2,1)} %get-tuple-element.118.refs_0_, bf16[4,144,512]{2,1,0:T(8,128)(2,1)} %copy-done, bf16[4,144,512]{2,1,0:T(8,128)(2,1)} %copy-done.1, ...), custom_call_target="tpu_custom_call" | custom-call | flops 1000000 | bytes 100 | tf_op jit(solution)/shard_map/plane_ffn/pallas_call | solution.py:471
  174.0 2.0 collective-permute-start.19
  177.1 1.7 collective-permute-start.21
  181.6 9.8 %input_grad.1.refs_4_ = f32[4,532,512]{2,1,0:T(8,128)} custom-call(bf16[144,512]{1,0:T(8,128)(2,1)} %get-tuple-element.127.refs_0_, f32[4,544,512]{2,1,0:T(8,128)} %get-tuple-element.128.refs_1_, bf16[4,256,640]{2,1,0:T(8,128)(2,1)} %get-tuple-element.129.refs_2_, bf16[4,544,256]{2,1,0:T(8,128)(2,1)} %get-tuple-element.130.refs_3_, ...), custom_call_target="tpu_custom_call" | custom-call | flops 10000000000 | bytes 1000000 | tf_op jit(solution)/shard_map/input_grad/pallas_call | solution.py:655
  193.4 1.9 plane_attn.1
  195.4 2.2 collective-permute-start.22
  199.3 7.1 %copy.50 = f32[4,532,512]{2,0,1:T(4,128)} copy(f32[4,532,512]{2,1,0:T(8,128)} %input_grad.1.refs_4_) | data formatting | bytes 8716288 | tf_op jit(solution)/shard_map/optimization_barrier | solution.py:775
  207.8 2.0 last.1.refs_0_
  213.2 5.7 %collective-permute-done.27.refs_3_ = bf16[208,512]{1,0:T(8,128)(2,1)S(1)} collective-permute-done((bf16[208,512]{1,0:T(8,128)(2,1)}, bf16[208,512]{1,0:T(8,128)(2,1)S(1)}, u32[]{:S(2)}, u32[]{:S(2)}) %collective-permute-start.27) | collective-permute-done | bytes 213024 | tf_op jit(solution)/shard_map/ppermute | solution.py:730
  223.8 4.4 %final.1 = (f32[512,512]{1,0:T(8,128)}, f32[512,512]{1,0:T(8,128)}, f32[128,512]{1,0:T(8,128)}, f32[128,512]{1,0:T(8,128)}, f32[128,512]{1,0:T(8,128)}, /*index=...) custom-call(s32[2]{0:T(128)} %pad_add_fusion.at_ref, ...), custom_call_target="tpu_custom_call" | custom-call | flops 3000000000 | bytes 300000 | tf_op jit(solution)/shard_map/final/pallas_call | solution.py:708
  (136 shorter events, 36.1 us)
Async XLA Ops:
  3.7 16.9 %collective-permute-start.2 = (bf16[144,512]{1,0:T(8,128)(2,1)}, bf16[144,512]{1,0:T(8,128)(2,1)S(1)}, u32[]{:S(2)}, u32[]{:S(2)}) collective-permute-start(bf16[144,512]{1,0:T(8,128)(2,1)} %prep.1.refs_8_), channel_id=1, source_target_pairs={{0,3},{1,0},{2,1},{3,2},{4,7},{5,4},{6,5},{7,6},{8,11},{9,8},{10,9... | collective-permute-start | bytes 442376 | tf_op jit(solution)/shard_map/ppermute | solution.py:733
  8.7 12.7 %collective-permute-start.1 = (bf16[144,512]{1,0:T(8,128)(2,1)}, bf16[144,512]{1,0:T(8,128)(2,1)S(1)}, u32[]{:S(2)}, u32[]{:S(2)}) collective-permute-start(bf16[144,512]{1,0:T(8,128)(2,1)} %prep.1.refs_8_), channel_id=1, source_target_pairs={{0,2},{1,3},{2,0},{3,1},{4,6},{5,7},{6,4},{7,5},{8,10},{9,11},{10,... | collective-permute-start | bytes 442376 | tf_op jit(solution)/shard_map/ppermute | solution.py:733
  8.7 12.7 %collective-permute-start = (bf16[144,512]{1,0:T(8,128)(2,1)}, bf16[144,512]{1,0:T(8,128)(2,1)S(1)}, u32[]{:S(2)}, u32[]{:S(2)}) collective-permute-start(bf16[144,512]{1,0:T(8,128)(2,1)} %prep.1.refs_8_), channel_id=1, source_target_pairs={{0,1},{1,2},{2,3},{3,0},{4,5},{5,6},{6,7},{7,4},{8,9},{9,10},{10,1... | collective-permute-start | bytes 442376 | tf_op jit(solution)/shard_map/ppermute | solution.py:733
  23.9 20.7 %collective-permute-start.5 = (bf16[3,128,512]{2,1,0:T(8,128)(2,1)}, bf16[3,128,512]{2,1,0:T(8,128)(2,1)S(1)}, u32[]{:S(2)}, u32[]{:S(2)}) collective-permute-start(bf16[3,128,512]{2,1,0:T(8,128)(2,1)} %get-tuple-element.102.refs_7_.refs_0_), channel_id=1, source_target_pairs={{0,24},{4,28},{8,16},{12,20},{16,8},{20,12},{24,0},{28,4},{1,25},{... | collective-permute-start | bytes 1179656 | tf_op jit(solution)/shard_map/ppermute | solution.py:730
  26.4 18.3 %collective-permute-start.4 = (bf16[3,128,512]{2,1,0:T(8,128)(2,1)}, bf16[3,128,512]{2,1,0:T(8,128)(2,1)S(1)}, u32[]{:S(2)}, u32[]{:S(2)}) collective-permute-start(bf16[3,128,512]{2,1,0:T(8,128)(2,1)} %get-tuple-element.102.refs_7_.refs_0_), channel_id=1, source_target_pairs={{0,16},{4,20},{8,24},{12,28},{16,0},{20,4},{24,8},{28,12},{1,17},{... | collective-permute-start | bytes 1179656 | tf_op jit(solution)/shard_map/ppermute | solution.py:730
  26.9 17.8 %collective-permute-start.3 = (bf16[3,128,512]{2,1,0:T(8,128)(2,1)}, bf16[3,128,512]{2,1,0:T(8,128)(2,1)S(1)}, u32[]{:S(2)}, u32[]{:S(2)}) collective-permute-start(bf16[3,128,512]{2,1,0:T(8,128)(2,1)} %get-tuple-element.102.refs_7_.refs_0_), channel_id=1, source_target_pairs={{0,8},{4,12},{8,0},{12,4},{16,24},{20,28},{24,16},{28,20},{1,9},{5... | collective-permute-start | bytes 1179656 | tf_op jit(solution)/shard_map/ppermute | solution.py:730
  44.8 2.9 %collective-permute-start.6 = (bf16[3,128,512]{2,1,0:T(8,128)(2,1)S(1)}, bf16[3,128,512]{2,1,0:T(8,128)(2,1)S(1)}, u32[]{:S(2)}, u32[]{:S(2)}) collective-permute-start(bf16[3,128,512]{2,1,0:T(8,128)(2,1)S(1)} %copy-done.18), channel_id=1, source_target_pairs={{0,4},{4,0},{8,12},{12,8},{16,20},{20,16},{24,28},{28,24},{1,5},{5... | collective-permute-start | bytes 1179656 | tf_op jit(solution)/shard_map/ppermute | solution.py:730
  108.4 22.0 %collective-permute-start.10 = (bf16[4,4,144,512]{3,2,1,0:T(8,128)(2,1)}, bf16[4,4,144,512]{3,2,1,0:T(8,128)(2,1)S(1)}, u32[]{:S(2)}, u32[]{:S(2)}) collective-permute-start(bf16[4,4,144,512]{3,2,1,0:T(8,128)(2,1)} %get-tuple-element.115), channel_id=1, source_target_pairs={{0,4},{4,0},{8,12},{12,8},{16,20},{20,16},{24,28},{28,24},{1,5},{5... | collective-permute-start | bytes 7077896 | tf_op jit(solution)/shard_map/ppermute | solution.py:730
  129.9 9.7 %collective-permute-start.11 = (bf16[4,4,32,512]{3,2,1,0:T(8,128)(2,1)}, bf16[4,4,32,512]{3,2,1,0:T(8,128)(2,1)S(1)}, u32[]{:S(2)}, u32[]{:S(2)}) collective-permute-start(bf16[4,4,32,512]{3,2,1,0:T(8,128)(2,1)} %get-tuple-element.119), channel_id=1, source_target_pairs={{0,4},{4,0},{8,12},{12,8},{16,20},{20,16},{24,28},{28,24},{1,5},{5... | collective-permute-start | bytes 1572872 | tf_op jit(solution)/shard_map/ppermute | solution.py:730
  136.1 27.8 %collective-permute-start.12 = (bf16[4,144,512]{2,1,0:T(8,128)(2,1)}, bf16[4,144,512]{2,1,0:T(8,128)(2,1)S(1)}, u32[]{:S(2)}, u32[]{:S(2)}) collective-permute-start(bf16[4,144,512]{2,1,0:T(8,128)(2,1)} %get-tuple-element.122), channel_id=1, source_target_pairs={{0,8},{4,12},{8,0},{12,4},{16,24},{20,28},{24,16},{28,20},{1,9},{5... | collective-permute-start | bytes 1769480 | tf_op jit(solution)/shard_map/ppermute | solution.py:730
  137.6 27.9 %collective-permute-start.13 = (bf16[4,144,512]{2,1,0:T(8,128)(2,1)}, bf16[4,144,512]{2,1,0:T(8,128)(2,1)S(1)}, u32[]{:S(2)}, u32[]{:S(2)}) collective-permute-start(bf16[4,144,512]{2,1,0:T(8,128)(2,1)} %get-tuple-element.123), channel_id=1, source_target_pairs={{0,16},{4,20},{8,24},{12,28},{16,0},{20,4},{24,8},{28,12},{1,17},{... | collective-permute-start | bytes 1769480 | tf_op jit(solution)/shard_map/ppermute | solution.py:730
  139.0 26.4 %collective-permute-start.14 = (bf16[4,144,512]{2,1,0:T(8,128)(2,1)}, bf16[4,144,512]{2,1,0:T(8,128)(2,1)S(1)}, u32[]{:S(2)}, u32[]{:S(2)}) collective-permute-start(bf16[4,144,512]{2,1,0:T(8,128)(2,1)} %get-tuple-element.124), channel_id=1, source_target_pairs={{0,24},{4,28},{8,16},{12,20},{16,8},{20,12},{24,0},{28,4},{1,25},{... | collective-permute-start | bytes 1769480 | tf_op jit(solution)/shard_map/ppermute | solution.py:730
  170.7 9.7 %collective-permute-start.16 = (bf16[4,64,512]{2,1,0:T(8,128)(2,1)}, bf16[4,64,512]{2,1,0:T(8,128)(2,1)S(1)}, u32[]{:S(2)}, u32[]{:S(2)}) collective-permute-start(bf16[4,64,512]{2,1,0:T(8,128)(2,1)} %get-tuple-element.135), channel_id=1, source_target_pairs={{0,8},{4,12},{8,0},{12,4},{16,24},{20,28},{24,16},{28,20},{1,9},{5... | collective-permute-start | bytes 786440 | tf_op jit(solution)/shard_map/ppermute | solution.py:730
  174.0 23.6 %collective-permute-start.19 = (bf16[144,512]{1,0:T(8,128)(2,1)}, bf16[144,512]{1,0:T(8,128)(2,1)S(1)}, u32[]{:S(2)}, u32[]{:S(2)}) collective-permute-start(bf16[144,512]{1,0:T(8,128)(2,1)} %get-tuple-element.140), channel_id=1, source_target_pairs={{0,3},{1,0},{2,1},{3,2},{4,7},{5,4},{6,5},{7,6},{8,11},{9,8},{10,9... | collective-permute-start | bytes 442376 | tf_op jit(solution)/shard_map/ppermute | solution.py:733
  176.0 30.4 %collective-permute-start.20 = (bf16[144,512]{1,0:T(8,128)(2,1)}, bf16[144,512]{1,0:T(8,128)(2,1)S(1)}, u32[]{:S(2)}, u32[]{:S(2)}) collective-permute-start(bf16[144,512]{1,0:T(8,128)(2,1)} %get-tuple-element.141), channel_id=1, source_target_pairs={{0,2},{1,3},{2,0},{3,1},{4,6},{5,7},{6,4},{7,5},{8,10},{9,11},{10,... | collective-permute-start | bytes 442376 | tf_op jit(solution)/shard_map/ppermute | solution.py:733
  177.1 29.2 %collective-permute-start.21 = (bf16[144,512]{1,0:T(8,128)(2,1)}, bf16[144,512]{1,0:T(8,128)(2,1)S(1)}, u32[]{:S(2)}, u32[]{:S(2)}) collective-permute-start(bf16[144,512]{1,0:T(8,128)(2,1)} %get-tuple-element.142), channel_id=1, source_target_pairs={{0,1},{1,2},{2,3},{3,0},{4,5},{5,6},{6,7},{7,4},{8,9},{9,10},{10,1... | collective-permute-start | bytes 442376 | tf_op jit(solution)/shard_map/ppermute | solution.py:733
  178.8 13.2 %collective-permute-start.17 = (bf16[4,64,512]{2,1,0:T(8,128)(2,1)S(1)}, bf16[4,64,512]{2,1,0:T(8,128)(2,1)S(1)}, u32[]{:S(2)}, u32[]{:S(2)}) collective-permute-start(bf16[4,64,512]{2,1,0:T(8,128)(2,1)S(1)} %copy-done.27), channel_id=1, source_target_pairs={{0,16},{4,20},{8,24},{12,28},{16,0},{20,4},{24,8},{28,12},{1,17},{... | collective-permute-start | bytes 786440 | tf_op jit(solution)/shard_map/ppermute | solution.py:730
  180.3 11.7 %collective-permute-start.18 = (bf16[4,64,512]{2,1,0:T(8,128)(2,1)S(1)}, bf16[4,64,512]{2,1,0:T(8,128)(2,1)S(1)}, u32[]{:S(2)}, u32[]{:S(2)}) collective-permute-start(bf16[4,64,512]{2,1,0:T(8,128)(2,1)S(1)} %copy-done.26), channel_id=1, source_target_pairs={{0,24},{4,28},{8,16},{12,20},{16,8},{20,12},{24,0},{28,4},{1,25},{... | collective-permute-start | bytes 786440 | tf_op jit(solution)/shard_map/ppermute | solution.py:730
  195.4 11.1 %collective-permute-start.22 = (bf16[64,512]{1,0:T(8,128)(2,1)}, bf16[64,512]{1,0:T(8,128)(2,1)S(1)}, u32[]{:S(2)}, u32[]{:S(2)}) collective-permute-start(bf16[64,512]{1,0:T(8,128)(2,1)} %get-tuple-element.143), channel_id=1, source_target_pairs={{0,3},{1,0},{2,1},{3,2},{4,7},{5,4},{6,5},{7,6},{8,11},{9,8},{10,9... | collective-permute-start | bytes 196616 | tf_op jit(solution)/shard_map/ppermute | solution.py:733
  197.5 8.9 %collective-permute-start.23 = (bf16[64,512]{1,0:T(8,128)(2,1)}, bf16[64,512]{1,0:T(8,128)(2,1)S(1)}, u32[]{:S(2)}, u32[]{:S(2)}) collective-permute-start(bf16[64,512]{1,0:T(8,128)(2,1)} %get-tuple-element.144), channel_id=1, source_target_pairs={{0,2},{1,3},{2,0},{3,1},{4,6},{5,7},{6,4},{7,5},{8,10},{9,11},{10,... | collective-permute-start | bytes 196616 | tf_op jit(solution)/shard_map/ppermute | solution.py:733
  197.6 8.9 %collective-permute-start.24 = (bf16[64,512]{1,0:T(8,128)(2,1)}, bf16[64,512]{1,0:T(8,128)(2,1)S(1)}, u32[]{:S(2)}, u32[]{:S(2)}) collective-permute-start(bf16[64,512]{1,0:T(8,128)(2,1)} %get-tuple-element.145), channel_id=1, source_target_pairs={{0,1},{1,2},{2,3},{3,0},{4,5},{5,6},{6,7},{7,4},{8,9},{9,10},{10,1... | collective-permute-start | bytes 196616 | tf_op jit(solution)/shard_map/ppermute | solution.py:733
  209.8 9.2 %collective-permute-start.27 = (bf16[208,512]{1,0:T(8,128)(2,1)}, bf16[208,512]{1,0:T(8,128)(2,1)S(1)}, u32[]{:S(2)}, u32[]{:S(2)}) collective-permute-start(bf16[208,512]{1,0:T(8,128)(2,1)} %last.1.refs_0_), channel_id=1, source_target_pairs={{0,24},{4,28},{8,16},{12,20},{16,8},{20,12},{24,0},{28,4},{1,25},{... | collective-permute-start | bytes 638984 | tf_op jit(solution)/shard_map/ppermute | solution.py:730
  210.2 10.1 %collective-permute-start.26 = (bf16[208,512]{1,0:T(8,128)(2,1)}, bf16[208,512]{1,0:T(8,128)(2,1)S(1)}, u32[]{:S(2)}, u32[]{:S(2)}) collective-permute-start(bf16[208,512]{1,0:T(8,128)(2,1)} %last.1.refs_0_), channel_id=1, source_target_pairs={{0,16},{4,20},{8,24},{12,28},{16,0},{20,4},{24,8},{28,12},{1,17},{... | collective-permute-start | bytes 638984 | tf_op jit(solution)/shard_map/ppermute | solution.py:730
  211.7 8.6 %collective-permute-start.25 = (bf16[208,512]{1,0:T(8,128)(2,1)}, bf16[208,512]{1,0:T(8,128)(2,1)S(1)}, u32[]{:S(2)}, u32[]{:S(2)}) collective-permute-start(bf16[208,512]{1,0:T(8,128)(2,1)} %last.1.refs_0_), channel_id=1, source_target_pairs={{0,8},{4,12},{8,0},{12,4},{16,24},{20,28},{24,16},{28,20},{1,9},{5... | collective-permute-start | bytes 638984 | tf_op jit(solution)/shard_map/ppermute | solution.py:730
  (46 other events, 162.2 us)
